TPU v7x, 256 devices: a whole 4x4x8 slice. The times are simulated.
256 devices in a mesh: dp: 4 (over y), seq: 2 (over core), expert: 32 (over x, z).
Axes of the slice: x: 4, y: 4, z: 8, core: 2. Of those that a mesh axis runs over, the one named last changes fastest.
Arguments:
- tokens: bfloat16 [4096, 3584], P('expert', 'dp'), may hold values from -6 to 6
- cotangent: bfloat16 [4096, 3584], P('expert', 'dp'), may hold values from -6 to 6
- expert_ids: int32 [4096, 8], P('expert'), may hold values from 0 to 63, all different within a row; in each aligned block of 128 rows (0 to 127, 128 to 255, ...) at most 24 rows name the same one
- gate_weights: float32 [4096, 8], P('expert'), may hold values from 0.08 to 0.8
- gate_proj: bfloat16 [64, 3584, 1024], P('expert', 'dp', 'seq'), may hold values from -0.09375 to 0.09375
- up_proj: bfloat16 [64, 3584, 1024], P('expert', 'dp', 'seq'), may hold values from -0.09375 to 0.09375
- down_proj: bfloat16 [64, 1024, 3584], P('expert', 'seq', 'dp'), may hold values from -0.1875 to 0.1875
Outputs:
- grad_tokens: bfloat16 [4096, 3584], P('expert', 'dp')
- grad_gate: bfloat16 [64, 3584, 1024], P('expert', 'dp', 'seq')
- grad_up: bfloat16 [64, 3584, 1024], P('expert', 'dp', 'seq')
- grad_down: bfloat16 [64, 1024, 3584], P('expert', 'seq', 'dp')
Inputs may be any that keep to these rules, and one draw needn't show every extreme that they name: `expert_ids`: each row names 8 different experts. Among the 128 tokens of one index of expert no expert is named by more than 24 of them, and in every draw some expert is named by exactly 24 tokens of some index.
All inputs are finite; a program needn't handle non-finite values.
Results may differ from a plain program's by a relative error of at most 0.0064.
Values may be sent and summed in bfloat16 or wider, within the bound.
No kernel may reach another device: no remote copies, remote signals or barrier semaphores. Data moves between devices by JAX's collectives and lax.ppermute only.
A program may use at most 128 MiB of HBM per device.

v0:
```python
import functools
import jax
import jax.numpy as jnp
from jax import lax
from jax.experimental import pallas as pl
from jax.experimental.pallas import tpu as pltpu
from jax.sharding import Mesh, PartitionSpec as P

BF = jnp.bfloat16
F32 = jnp.float32
NX, NZ, NY = 4, 8, 4
TB = 128
CAP = 24
QR = 48
MR = 192
DC = 896
FH = 512
META = 128
CHUNKS = ((0,), (1, 3), (2,))
VMEM = pl.BlockSpec(memory_space=pltpu.VMEM)
SMEM = pl.BlockSpec(memory_space=pltpu.SMEM)
NN = (((1,), (0,)), ((), ()))
NT = (((1,), (1,)), ((), ()))
TN = (((0,), (0,)), ((), ()))


def dot(a, b, dims=NN):
    return lax.dot_general(a, b, dims, preferred_element_type=F32)


ANY = pl.BlockSpec(memory_space=pl.ANY)


class Queue:
    def __init__(self):
        self.last = None

    def __call__(
        self, body, outs, ins, scratch=(), name=None, after=(), hand=(), hbm=False, limit=48, free=False
    ):
        waits = list(after) + ([] if free or self.last is None else [self.last])
        n, k, h, m = len(ins), len(waits), len(hand), len(outs)

        def run(*refs):
            body(*refs[:n], *refs[n + k + h : n + k + h + m], *refs[n + k + 2 * h + m :])

        done = pl.pallas_call(
            run,
            out_shape=[jax.ShapeDtypeStruct(s, t) for s, t in outs]
            + [jax.ShapeDtypeStruct(v.shape, v.dtype) for v in hand],
            in_specs=[SMEM if v.shape == (9,) else ANY if hbm else VMEM for v in ins]
            + [ANY] * (k + h),
            out_specs=[VMEM] * m + [ANY] * h,
            scratch_shapes=[pltpu.VMEM(*v) if isinstance(v, tuple) else v for v in scratch],
            input_output_aliases={n + k + i: m + i for i in range(h)},
            compiler_params=pltpu.CompilerParams(vmem_limit_bytes=limit * 2**20),
            cost_estimate=pl.CostEstimate(flops=1, bytes_accessed=1, transcendentals=0),
            name=name,
        )(*ins, *waits, *hand)
        if not free:
            self.last = done[0]
        return done


def first(y, s):
    return y ^ 1 if s == 0 else 3 - y


def second(y, s):
    return 3 - y if s == 0 else y ^ 1


def to_first(v):
    return lax.ppermute(
        v, ("dp", "seq"), [(y * 2 + s, first(y, s) * 2 + s) for y in range(NY) for s in range(2)]
    )


def to_second(v):
    return lax.ppermute(
        v, ("dp", "seq"), [(y * 2 + s, second(y, s) * 2 + s) for y in range(NY) for s in range(2)]
    )


def along_z(v, far):
    pairs = [(z, (z + far) % NZ) for z in range(NZ)]
    pairs += [(NZ + z, NZ + (z - far) % NZ) for z in range(NZ)]
    return lax.ppermute(v, ("seq", "ez"), pairs)


def opposite(v):
    pairs = [(z, (z + 2) % NZ) for z in range(0, NZ, 2)]
    pairs += [(NZ + z, NZ + (z - 2) % NZ) for z in range(1, NZ, 2)]
    return lax.ppermute(v, ("seq", "ez"), pairs)


def swap_opposite(v):
    pairs = [(z, NZ + z) if z % 2 == 0 else (NZ + z, z) for z in range(NZ)]
    return lax.ppermute(v, ("seq", "ez"), pairs)


def along_x(v, far):
    return lax.ppermute(v, "ex", [(x, (x + far) % NX) for x in range(NX)])


def swap(v):
    return lax.ppermute(v, "seq", [(0, 1), (1, 0)])


def copy_all(pairs, sems):
    copies = [pltpu.make_async_copy(a, b, sems.at[i]) for i, (a, b) in enumerate(pairs)]
    for copy in copies:
        copy.start()
    for copy in copies:
        copy.wait()


def half_of(gate, up, down, t, out):
    return (
        (gate.at[t], out.at[:DC]),
        (up.at[t], out.at[DC : 2 * DC]),
        (down.at[t, :, :FH], out.at[2 * DC : 2 * DC + FH]),
        (down.at[t, :, FH:], out.at[2 * DC + FH :, : DC - FH]),
    )


def pack(info, tokens, cot, ids, gates, gate, up, down, out, weights, numbers, scale, meta, sems):
    copies = [
        pltpu.make_async_copy(a, b, sems.at[i])
        for i, (a, b) in enumerate(
            (
                (ids, numbers),
                (gates, scale),
                (tokens, out.at[:, :DC]),
                (cot, out.at[:, DC : 2 * DC]),
                *half_of(gate, up, down, 1 - info[8], weights),
            )
        )
    ]
    for copy in copies:
        copy.start()
    meta[...] = jnp.zeros_like(meta)
    weights[2 * DC + FH :, DC - FH :] = jnp.zeros((FH, 2 * FH - DC), BF)
    copies[0].wait()
    copies[1].wait()
    high = scale[...].astype(BF).astype(F32)
    middle = (scale[...] - high).astype(BF).astype(F32)
    meta[0:8] = numbers[...].astype(F32)
    meta[8:16] = high
    meta[16:24] = middle
    meta[24:32] = (scale[...] - high) - middle
    out[:, 2 * DC :] = jnp.transpose(meta[...]).astype(BF)
    for copy in copies[2:]:
        copy.wait()


def pack_own(info, gate, up, down, out, sems):
    copy_all(half_of(gate, up, down, info[8], out), sems)
    out[2 * DC + FH :, DC - FH :] = jnp.zeros((FH, 2 * FH - DC), BF)


def place_grads(info, got, gate, up, down, token, gate_out, up_out, down_out, sems):
    t = 1 - info[8]
    copy_all(
        (
            (got.at[:DC], gate_out.at[t]),
            (got.at[DC : 2 * DC], up_out.at[t]),
            (got.at[2 * DC : 2 * DC + FH], down_out.at[t, :, :FH]),
            (got.at[2 * DC + FH :, : DC - FH], down_out.at[t, :, FH:]),
        ),
        sems,
    )


def bring_home(info, home, h1, h2, h3, h4, out):
    out[...] = home[...] + h1[...].astype(F32) + h2[...].astype(F32) + h3[...].astype(F32)
    at = pl.ds(pl.multiple_of(info[8] * (TB // 2), TB // 2), TB // 2)
    out[at] = out[at] + h4[...].astype(F32)


def finish(mine, other, out, token):
    token[...] = jnp.zeros_like(token)
    out[...] = (mine[...] + other[...]).astype(BF)


def put_down(out, down):
    out[2 * DC : 2 * DC + FH] = down[:, :FH]
    out[2 * DC + FH :, : DC - FH] = down[:, FH:]
    out[2 * DC + FH :, DC - FH :] = jnp.zeros((FH, 2 * FH - DC), BF)


def marks(slots, hot, q):
    masks = []
    for d in range(NX):
        for b in (2 * q, 2 * q + 1):
            at = d * NZ + b
            row = slots[at : at + 1, :]
            mask = lax.broadcasted_iota(jnp.int32, (QR, TB), 0).astype(F32) == row
            side = (b % 2) * TB
            hot[d * QR : (d + 1) * QR, side : side + TB] = mask.astype(F32).astype(BF)
            masks.append((at, mask))
    return masks


def pick(info, own, r1, r2, r3, r4, s4, s1, s2, s3, m0, m1, m2, m3, slots, rows, taken, gates, hot):
    for b, block in enumerate((own, r1, r2, r3, r4, s1, s2, s3)):
        at = slice(b * TB, (b + 1) * TB)
        if b == 4:
            rows[at] = r4[:, : 2 * DC] + s4[:, : 2 * DC]
            meta = r4[:, 2 * DC :] + s4[:, 2 * DC :]
        else:
            rows[at] = block[:, : 2 * DC]
            meta = block[:, 2 * DC :]
        turned = jnp.transpose(meta.astype(F32))
        ids = turned[0:8]
        gate = turned[8:16] + turned[16:24] + turned[24:32]
        for d in range(NX):
            named = ids == info[d].astype(F32)
            at = slice(d * NZ + b, d * NZ + b + 1)
            taken[at, :] = jnp.sum(named.astype(F32), axis=0, keepdims=True)
            gates[at, :] = jnp.sum(jnp.where(named, gate, 0.0), axis=0, keepdims=True)
    upper = lax.broadcasted_iota(jnp.int32, (TB, TB), 0) < lax.broadcasted_iota(
        jnp.int32, (TB, TB), 1
    )
    rank = dot(taken[...].astype(BF), upper.astype(F32).astype(BF))
    odd = lax.broadcasted_iota(jnp.int32, (NX * NZ, TB), 0) % 2
    slots[...] = jnp.where(taken[...] > 0.5, rank + (odd * CAP).astype(F32), -1.0)
    for q in range(4):
        found = [
            jnp.where(mask, gates[at : at + 1, :], 0.0) for at, mask in marks(slots, hot, q)
        ]
        tokens = slice(2 * q * TB, 2 * (q + 1) * TB)
        x = dot(hot[...], rows[tokens, :DC]).astype(BF)
        w = dot(hot[...], rows[tokens, DC:])
        place = pl.ds(pl.multiple_of(info[4 + q], QR), QR)
        for d, out in enumerate((m0, m1, m2, m3)):
            gate = jnp.sum(found[2 * d] + found[2 * d + 1], axis=1, keepdims=True)
            part = slice(d * QR, (d + 1) * QR)
            out[place, :DC] = x[part]
            out[place, DC:] = (gate * w[part]).astype(BF)


def combine(info, slots, b0, b1, b2, b3, own, mine, theirs, rows, hot, far):
    half = TB // 2
    for q in range(4):
        marks(slots, hot, q)
        place = pl.ds(pl.multiple_of(info[4 + q], QR), QR)
        for d, ref in enumerate((b0, b1, b2, b3)):
            rows[d * QR : (d + 1) * QR] = ref[place]
        for b in (2 * q, 2 * q + 1):
            side = (b % 2) * TB
            part = dot(hot[:, side : side + TB], rows[...], TN)
            if b == 0:
                own[...] = part
            elif b < 4:
                mine[(b - 1) * TB : b * TB] = part
            elif b == 4:
                far[...] = part
                mine[3 * TB :] = far[pl.ds(pl.multiple_of(info[8] * half, half), half)]
                theirs[3 * TB :] = far[
                    pl.ds(pl.multiple_of((1 - info[8]) * half, half), half)
                ].astype(BF)
            else:
                theirs[(b - 5) * TB : (b - 4) * TB] = part.astype(BF)


def join(mine, got, o1, o2, o3, o4):
    for i, out in enumerate((o1, o2, o3)):
        at = slice(i * TB, (i + 1) * TB)
        out[...] = (mine[at] + got[at].astype(F32)).astype(BF)
    o4[...] = (mine[384:448] + got[384:448].astype(F32)).astype(BF)


def by_quarter(dst, refs, start=0):
    n = len(refs)
    for q in range(4):
        for i, ref in enumerate(refs):
            dst[start + (q * n + i) * QR : start + (q * n + i + 1) * QR] = ref[
                q * QR : (q + 1) * QR
            ]


def products(n, *refs):
    messages, (own, other, keep, send, rows) = refs[:n], refs[n:]
    by_quarter(rows, messages)
    x, w = rows[:, :DC], rows[:, DC:]
    half = n * 2 * QR
    down = 2 * DC
    for at, part in ((0, own), (FH, other)):
        for k, v in (
            (0, dot(x, part[:DC])),
            (1, dot(x, part[DC:down])),
            (
                2,
                dot(w[:, :FH], part[down : down + FH], NT)
                + dot(w[:, FH:], part[down + FH :, : DC - FH], NT),
            ),
        ):
            keep[k, :, at : at + FH] = v[:half]
            send[k, :, at : at + FH] = v[half:].astype(BF)


def halve(keep, got, mine, send):
    m = keep.shape[-2] // 2
    mine[...] = keep[..., :m, :] + got[..., :m, :].astype(F32)
    send[...] = (keep[..., m:, :] + got[..., m:, :].astype(F32)).astype(BF)


def terms(keep, got, out):
    g = keep[0] + got[0].astype(F32)
    u = keep[1] + got[1].astype(F32)
    h = keep[2] + got[2].astype(F32)
    s = jax.nn.sigmoid(g)
    act = g * s
    out[0] = (act * u).astype(BF)
    out[1] = (h * u * s * (1.0 + g * (1.0 - s))).astype(BF)
    out[2] = (h * act).astype(BF)


def back_rows(n, a0, a1, a2, a3, own, other, *refs):
    outs, (dg, du) = refs[:n], refs[n:]
    m = n * QR
    for q, a in enumerate((a0, a1, a2, a3)):
        dg[q * m : (q + 1) * m] = a[1]
        du[q * m : (q + 1) * m] = a[2]
    total = dot(dg[:, :FH], own[:DC], NT) + dot(dg[:, FH:], other[:DC], NT)
    total = total + dot(du[:, :FH], own[DC : 2 * DC], NT) + dot(du[:, FH:], other[DC : 2 * DC], NT)
    total = total.astype(BF)
    for q in range(4):
        for i, out in enumerate(outs):
            out[q * QR : (q + 1) * QR] = total[(q * n + i) * QR : (q * n + i + 1) * QR]


def weight_grads(info, *refs):
    messages, parts = refs[:4], refs[4 : 4 + 4 * len(CHUNKS)]
    token, gate, up, down, send, rows, cols = refs[4 + 4 * len(CHUNKS) :]
    s = info[8]
    token[...] = jnp.zeros_like(token)
    start = 0
    for c, chunk in enumerate(CHUNKS):
        n = len(chunk)
        by_quarter(rows, [messages[d] for d in chunk], start)
        for q in range(4):
            at = start + q * n * QR
            cols[:, at : at + n * QR] = parts[4 * c + q][...]
        start += n * MR
    x, w = rows[:, :DC], rows[:, DC:]
    down[s] = dot(cols[0, :, :FH], w, TN).astype(BF)
    put_down(send, dot(cols[0, :, FH:], w, TN).astype(BF))
    gate[s] = dot(x, cols[1, :, :FH], TN).astype(BF)
    send[:DC] = dot(x, cols[1, :, FH:], TN).astype(BF)
    up[s] = dot(x, cols[2, :, :FH], TN).astype(BF)
    send[DC : 2 * DC] = dot(x, cols[2, :, FH:], TN).astype(BF)


def on_device(tokens, cotangent, expert_ids, gate_weights, gate_proj, up_proj, down_proj):
    y, s = lax.axis_index("dp"), lax.axis_index("seq")
    x, z = lax.axis_index("ex"), lax.axis_index("ez")
    p1 = jnp.where(s == 0, y ^ 1, 3 - y)
    p2 = jnp.where(s == 0, 3 - y, y ^ 1)
    experts = [2 * (((x + d) % NX) * NZ + z) + s for d in range(NX)]
    bases = [
        QR * jnp.where(q == y, 0, jnp.where(q == p2, 1, jnp.where(q == p1, 2, 3)))
        for q in range(4)
    ]
    info = jnp.stack([jnp.asarray(v, jnp.int32) for v in [*experts, *bases, s]])

    queue = Queue()
    block, token = ((TB, DC), BF), ((8, TB), F32)

    weights = ((2 * DC + 2 * FH, FH), BF)
    message = ((MR, 2 * DC), BF)
    width = 2 * DC + META

    packed, others = queue(
        pack,
        [((TB, width), BF), weights],
        (
            info,
            tokens,
            cotangent,
            expert_ids.T,
            gate_weights.T,
            gate_proj,
            up_proj,
            down_proj,
        ),
        [
            ((8, TB), jnp.int32),
            ((8, TB), F32),
            ((META, TB), F32),
            pltpu.SemaphoreType.DMA((8,)),
        ],
        name="pack",
        hbm=True,
        limit=60,
    )
    r1, r2 = along_z(packed, 1), along_z(packed, 2)
    own_weights, r1 = queue(
        pack_own,
        [weights],
        (info, gate_proj, up_proj, down_proj),
        [pltpu.SemaphoreType.DMA((4,))],
        name="pack_own",
        hand=(r1,),
        hbm=True,
        limit=60,
        free=True,
    )
    r3, r4 = along_z(r2, 1), opposite(r2)
    others = swap(others)
    *messages, slots = queue(
        pick,
        [message] * 4 + [((32, TB), F32)],
        (info, packed, r1, r2, r3, r4, swap_opposite(r4), swap(r1), swap(r2), swap(r3)),
        [((1024, 2 * DC), BF), ((32, TB), F32), ((32, TB), F32), ((MR, 2 * TB), BF)],
        name="pick",
    )
    messages = [m if d == 0 else along_x(m, d) for d, m in enumerate(messages)]

    count = len(CHUNKS)
    sums, parts, returned = [None] * count, [None] * count, [None] * NX

    def multiply(c, *after):
        chunk = CHUNKS[c]
        n = len(chunk)
        keep, send = queue(
            functools.partial(products, n),
            [((3, n * 2 * QR, 1024), F32), ((3, n * 2 * QR, 1024), BF)],
            (*[messages[d] for d in chunk], own_weights, others),
            [((n * MR, 2 * DC), BF)],
            after=after,
            name="products",
        )
        sums[c] = keep, to_first(send)

    def reduce(c, *after):
        m = len(CHUNKS[c]) * QR
        keep, send = queue(
            halve, [((3, m, 1024), F32), ((3, m, 1024), BF)], sums[c], after=after, name="halve"
        )
        sums[c] = keep, to_second(send)

    def spread(c, *after):
        m = len(CHUNKS[c]) * QR
        [own] = queue(terms, [((3, m, 1024), BF)], sums[c], after=after, name="terms")
        a1, a2 = to_second(own), to_first(own)
        parts[c] = [own, a1, a2, to_first(a1)]

    def back(c, *after):
        chunk = CHUNKS[c]
        n = len(chunk)
        rows = queue(
            functools.partial(back_rows, n),
            [((MR, DC), BF)] * n,
            (*parts[c], own_weights, others),
            [((n * MR, 1024), BF)] * 2,
            after=after,
            name="back_rows",
        )
        for d, r in zip(chunk, rows):
            returned[d] = r if d == 0 else along_x(r, NX - d)

    multiply(0)
    reduce(0)
    multiply(1)
    multiply(2, sums[0][1])
    reduce(1)
    reduce(2)
    spread(1)
    spread(2)
    spread(0, *parts[1][:3])
    back(1, *parts[2][:3])
    back(2, *parts[0][:3])
    back(0, returned[1], returned[3])

    home, mine, theirs = queue(
        combine,
        [((TB, DC), F32), ((448, DC), F32), ((448, DC), BF)],
        (info, slots, *returned),
        [((MR, DC), BF), ((MR, 2 * TB), BF), ((TB, DC), F32)],
        name="combine",
    )
    homeward = queue(
        join,
        [block] * 3 + [((TB // 2, DC), BF)],
        (mine, swap(theirs)),
        name="join",
    )
    homed = [along_z(v, -far) for v, far in zip(homeward, (1, 2, 3, 4))]

    _, grad_gate, grad_up, grad_down, send = queue(
        weight_grads,
        [token, ((2, DC, FH), BF), ((2, DC, FH), BF), ((2, FH, DC), BF), weights],
        (info, *messages, *[a for part in parts for a in part]),
        [((4 * MR, 2 * DC), BF), ((3, 4 * MR, 1024), BF)],
        name="weight_grads",
    )
    total, send = queue(
        bring_home, [((TB, DC), F32)], (info, home, *homed), hand=(send,), name="bring_home"
    )
    grad_tokens, last = queue(finish, [block, token], (total, swap(total)), name="finish")
    shape = jax.ShapeDtypeStruct
    grad_gate, grad_up, grad_down = pl.pallas_call(
        place_grads,
        out_shape=[shape(v.shape, BF) for v in (grad_gate, grad_up, grad_down)],
        in_specs=[SMEM, VMEM] + [ANY] * 4,
        out_specs=[ANY] * 3,
        scratch_shapes=[pltpu.SemaphoreType.DMA((4,))],
        input_output_aliases={2: 0, 3: 1, 4: 2},
        compiler_params=pltpu.CompilerParams(vmem_limit_bytes=48 * 2**20),
        cost_estimate=pl.CostEstimate(flops=0, bytes_accessed=6_000_000, transcendentals=0),
        name="place_grads",
    )(info, swap(send), grad_gate, grad_up, grad_down, last)
    return grad_tokens, grad_gate, grad_up, grad_down


def solution(mesh):
    parts = Mesh(mesh.devices.reshape(NY, 2, NX, NZ), ("dp", "seq", "ex", "ez"))
    expert = ("ex", "ez")
    in_specs = (
        P(expert, "dp"),
        P(expert, "dp"),
        P(expert, None),
        P(expert, None),
        P(expert, "dp", "seq"),
        P(expert, "dp", "seq"),
        P(expert, "seq", "dp"),
    )
    out_specs = (
        P(expert, "dp"),
        P(expert, "dp", "seq"),
        P(expert, "dp", "seq"),
        P(expert, "seq", "dp"),
    )
    return jax.shard_map(
        on_device, mesh=parts, in_specs=in_specs, out_specs=out_specs, check_vma=False
    )
```

profile of v0, /device:TPU:33, one launch (start us, length us, event | category | flops | bytes accessed | tf_op | source)
XLA Modules:
  0.0 217.1 jit_solution(17498940621357112974)
XLA Ops:
  0.7 0.7 stack.39.refs_0_.info
  1.4 4.5 %pack.1 = (bf16[128,1920]{1,0:T(8,128)(2,1)}, bf16[2816,512]{1,0:T(8,128)(2,1)}) custom-call(s32[9]{0:T(128)} %stack.39.refs_0_.info, bf16[128,896]{1,0:T(8,128)(2,1)} %refs_1_.2, bf16[128,896]{1,0:T(8,128)(2,1)} %refs_2_.2, s32[8,128]{1,0:T(8,128)} %bitcast.11, f32[8,128]{1,0:T(8,128)} %bitcast.12, bf16[2,896,512]{2,1,0:T(8,128)(2,1)} %refs_1_.3, ...), custom_call_target="tpu_custom_call" | custom-call | flops 1 | bytes 1 | tf_op jit(solution)/shard_map/pack/pallas_call | solution.py:47
  5.9 0.8 collective-permute-start.8
  6.7 5.1 %collective-permute-start.1 = (bf16[128,1920]{1,0:T(8,128)(2,1)}, bf16[128,1920]{1,0:T(8,128)(2,1)S(1)}, u32[]{:S(2)}, u32[]{:S(2)}) collective-permute-start(bf16[128,1920]{1,0:T(8,128)(2,1)} %get-tuple-element.46.refs_1_.refs_10_), channel_id=1, source_target_pairs={{0,2},{1,3},{2,4},{3,5},{4,6},{5,7},{6,0},{7,1},{32,38},{33,39},{3... | collective-permute-start | bytes 1474568 | tf_op jit(solution)/shard_map/ppermute | solution.py:88
  11.8 0.7 collective-permute-start
  12.5 10.3 %collective-permute-done.1.refs_3_ = bf16[128,1920]{1,0:T(8,128)(2,1)S(1)} collective-permute-done((bf16[128,1920]{1,0:T(8,128)(2,1)}, bf16[128,1920]{1,0:T(8,128)(2,1)S(1)}, u32[]{:S(2)}, u32[]{:S(2)}) %collective-permute-start.1) | collective-permute-done | bytes 491552 | tf_op jit(solution)/shard_map/ppermute | solution.py:88
  22.8 5.9 %collective-permute-start.3 = (bf16[128,1920]{1,0:T(8,128)(2,1)S(1)}, bf16[128,1920]{1,0:T(8,128)(2,1)S(1)}, u32[]{:S(2)}, u32[]{:S(2)}) collective-permute-start(bf16[128,1920]{1,0:T(8,128)(2,1)S(1)} %collective-permute-done.1.refs_3_), channel_id=1, source_target_pairs={{0,2},{2,4},{4,6},{6,0},{33,39},{35,33},{37,35},{39,37},{8,10},{10... | collective-permute-start | bytes 1474568 | tf_op jit(solution)/shard_map/ppermute | solution.py:94
  28.8 0.8 copy-done.7
  29.6 4.0 %pack_own.1 = (bf16[2816,512]{1,0:T(8,128)(2,1)}, bf16[128,1920]{1,0:T(8,128)(2,1)}) custom-call(s32[9]{0:T(128)} %stack.39.refs_0_.info, bf16[2,896,512]{2,1,0:T(8,128)(2,1)} %refs_1_.3, bf16[2,896,512]{2,1,0:T(8,128)(2,1)} %refs_2_.3, bf16[2,512,896]{2,1,0:T(8,128)(2,1)} %refs_3_.1, bf16[128,1920]{1,0:T(8,128)(2,1)} %copy-done.7), custom_call_target="tpu_custom_call", output_to_operand_aliasing={{1}: (4, {})} | custom-call | flops 1 | bytes 1 | tf_op jit(solution)/shard_map/pack_own/pallas_call | solution.py:47
  33.6 2.9 %collective-permute-start.5 = (bf16[128,1920]{1,0:T(8,128)(2,1)}, bf16[128,1920]{1,0:T(8,128)(2,1)S(1)}, u32[]{:S(2)}, u32[]{:S(2)}) collective-permute-start(bf16[128,1920]{1,0:T(8,128)(2,1)} %get-tuple-element.47.refs_2_), channel_id=1, source_target_pairs={{0,32},{32,0},{1,33},{33,1},{2,34},{34,2},{3,35},{35,3},{4,36},{36... | collective-permute-start | bytes 1474568 | tf_op jit(solution)/shard_map/ppermute | solution.py:107
  36.6 2.5 %collective-permute-start.4 = (bf16[128,1920]{1,0:T(8,128)(2,1)S(1)}, bf16[128,1920]{1,0:T(8,128)(2,1)S(1)}, u32[]{:S(2)}, u32[]{:S(2)}) collective-permute-start(bf16[128,1920]{1,0:T(8,128)(2,1)S(1)} %collective-permute-done.3.refs_5_), channel_id=1, source_target_pairs={{0,32},{33,1},{2,34},{35,3},{4,36},{37,5},{6,38},{39,7},{8,40},{41... | collective-permute-start | bytes 1474568 | tf_op jit(solution)/shard_map/ppermute | solution.py:99
  39.1 0.6 collective-permute-done.2.refs_4_
  39.7 0.8 collective-permute-start.7
  40.5 1.4 collective-permute-done.7.refs_9_
  42.0 1.0 copy-done.8
  43.0 2.9 %pick.1 = (bf16[192,1792]{1,0:T(8,128)(2,1)S(1)}, bf16[192,1792]{1,0:T(8,128)(2,1)S(1)}, bf16[192,1792]{1,0:T(8,128)(2,1)}, bf16[192,1792]{1,0:T(8,128)(2,1)}, f32[32,128]{1,0:T(8,128)S(1)}) custom-call(s32[9]{0:T(128)S(1)} %copy-done.9, bf16[128,1920]{1,0:T(8,128)(2,1)S(1)} %copy-done.6, bf16[128,1920]{1,0:T(8,128)(2,1)S(1)} %copy-done.8, ...), custom_call_target="tpu_custom_call" | custom-call | flops 1 | bytes 1 | tf_op jit(solution)/shard_map/pick/pallas_call | solution.py:47
  46.0 1.2 collective-permute-start.11
  47.2 1.5 collective-permute-start.12
  48.6 3.4 %products.3 = (f32[3,96,1024]{2,1,0:T(8,128)S(1)}, bf16[3,96,1024]{2,1,0:T(8,128)(2,1)S(1)}) custom-call(bf16[192,1792]{1,0:T(8,128)(2,1)S(1)} %get-tuple-element.49.refs_0_.refs_3_.refs_1_, bf16[2816,512]{1,0:T(8,128)(2,1)S(1)} %copy-done, bf16[2816,512]{1,0:T(8,128)(2,1)} %collective-permute-done.8.refs_2_.refs_3_.refs_5_, ...), custom_call_target="tpu_custom_call" | custom-call | flops 1 | bytes 1 | tf_op jit(solution)/shard_map/products/pallas_call | solution.py:47
  52.1 2.8 %collective-permute-start.9 = (bf16[3,96,1024]{2,1,0:T(8,128)(2,1)S(1)}, bf16[3,96,1024]{2,1,0:T(8,128)(2,1)S(1)}, u32[]{:S(2)}, u32[]{:S(2)}) collective-permute-start(bf16[3,96,1024]{2,1,0:T(8,128)(2,1)S(1)} %get-tuple-element.53), channel_id=1, source_target_pairs={{0,64},{32,224},{64,0},{96,160},{128,192},{160,96},{192,128},{224,... | collective-permute-start | bytes 1769480 | tf_op jit(solution)/shard_map/ppermute | solution.py:74
  54.9 7.6 %collective-permute-done.9.refs_1_ = bf16[3,96,1024]{2,1,0:T(8,128)(2,1)S(1)} collective-permute-done((bf16[3,96,1024]{2,1,0:T(8,128)(2,1)S(1)}, bf16[3,96,1024]{2,1,0:T(8,128)(2,1)S(1)}, u32[]{:S(2)}, u32[]{:S(2)}) %collective-permute-start.9) | collective-permute-done | bytes 589856 | tf_op jit(solution)/shard_map/ppermute | solution.py:74
  62.6 1.3 collective-permute-done.11.refs_0_.refs_2_
  63.8 5.8 %products.4 = (f32[3,192,1024]{2,1,0:T(8,128)S(1)}, bf16[3,192,1024]{2,1,0:T(8,128)(2,1)S(1)}) custom-call(bf16[192,1792]{1,0:T(8,128)(2,1)S(1)} %collective-permute-done.11.refs_0_.refs_2_, bf16[192,1792]{1,0:T(8,128)(2,1)S(1)} %collective-permute-done.12.refs_1_.refs_4_, bf16[2816,512]{1,0:T(8,128)(2,1)} %get-tuple-element.50.refs_1_.refs_2_.refs_4_, ...), custom_call_target="tpu_custom_call" | custom-call | flops 1 | bytes 1 | tf_op jit(solution)/shard_map/products/pallas_call | solution.py:47
  69.7 2.8 %collective-permute-start.13 = (bf16[3,192,1024]{2,1,0:T(8,128)(2,1)S(1)}, bf16[3,192,1024]{2,1,0:T(8,128)(2,1)S(1)}, u32[]{:S(2)}, u32[]{:S(2)}) collective-permute-start(bf16[3,192,1024]{2,1,0:T(8,128)(2,1)S(1)} %get-tuple-element.59), channel_id=1, source_target_pairs={{0,64},{32,224},{64,0},{96,160},{128,192},{160,96},{192,128},{224,... | collective-permute-start | bytes 3538952 | tf_op jit(solution)/shard_map/ppermute | solution.py:74
  72.5 2.1 collective-permute-start.14
  74.6 16.4 %collective-permute-done.14.refs_0_.refs_3_ = bf16[192,1792]{1,0:T(8,128)(2,1)S(1)} collective-permute-done((bf16[192,1792]{1,0:T(8,128)(2,1)S(1)}, bf16[192,1792]{1,0:T(8,128)(2,1)S(1)}, u32[]{:S(2)}, u32[]{:S(2)}) %collective-permute-start.14) | collective-permute-done | bytes 688160 | tf_op jit(solution)/shard_map/ppermute | solution.py:103
  91.0 4.5 %products.5 = (f32[3,96,1024]{2,1,0:T(8,128)S(1)}, bf16[3,96,1024]{2,1,0:T(8,128)(2,1)S(1)}) custom-call(bf16[192,1792]{1,0:T(8,128)(2,1)S(1)} %collective-permute-done.14.refs_0_.refs_3_, bf16[2816,512]{1,0:T(8,128)(2,1)} %get-tuple-element.50.refs_1_.refs_2_.refs_4_, bf16[2816,512]{1,0:T(8,128)(2,1)} %collective-permute-done.8.refs_2_.refs_3_.refs_5_, ...), custom_call_target="tpu_custom_call" | custom-call | flops 1 | bytes 1 | tf_op jit(solution)/shard_map/products/pallas_call | solution.py:47
  95.7 1.9 halve.4
  97.7 11.1 %collective-permute-done.16.refs_1_ = bf16[3,96,1024]{2,1,0:T(8,128)(2,1)S(1)} collective-permute-done((bf16[3,96,1024]{2,1,0:T(8,128)(2,1)S(1)}, bf16[3,96,1024]{2,1,0:T(8,128)(2,1)S(1)}, u32[]{:S(2)}, u32[]{:S(2)}) %collective-permute-start.16) | collective-permute-done | bytes 589856 | tf_op jit(solution)/shard_map/ppermute | solution.py:74
  108.9 3.3 %collective-permute-done.15.refs_1_ = bf16[3,96,1024]{2,1,0:T(8,128)(2,1)S(1)} collective-permute-done((bf16[3,96,1024]{2,1,0:T(8,128)(2,1)S(1)}, bf16[3,96,1024]{2,1,0:T(8,128)(2,1)S(1)}, u32[]{:S(2)}, u32[]{:S(2)}) %collective-permute-start.15) | collective-permute-done | bytes 589856 | tf_op jit(solution)/shard_map/ppermute | solution.py:80
  112.2 0.3 terms.3.refs_2_.refs_0_.refs_9_
  112.6 1.5 collective-permute-start.19
  114.1 9.7 %collective-permute-done.17.refs_3_.refs_1_.refs_10_ = bf16[3,96,1024]{2,1,0:T(8,128)(2,1)S(1)} collective-permute-done((bf16[3,96,1024]{2,1,0:T(8,128)(2,1)S(1)}, bf16[3,96,1024]{2,1,0:T(8,128)(2,1)S(1)}, u32[]{:S(2)}, u32[]{:S(2)}) %collective-permute-start.17) | collective-permute-done | bytes 589856 | tf_op jit(solution)/shard_map/ppermute | solution.py:80
  123.8 6.3 %collective-permute-done.19.refs_1_ = bf16[3,48,1024]{2,1,0:T(8,128)(2,1)S(1)} collective-permute-done((bf16[3,48,1024]{2,1,0:T(8,128)(2,1)S(1)}, bf16[3,48,1024]{2,1,0:T(8,128)(2,1)S(1)}, u32[]{:S(2)}, u32[]{:S(2)}) %collective-permute-start.19) | collective-permute-done | bytes 294944 | tf_op jit(solution)/shard_map/ppermute | solution.py:80
  130.1 0.1 terms.4.refs_5_.refs_6_.refs_0_.refs_13_
  130.3 0.4 collective-permute-start.24
  130.6 0.8 collective-permute-start.25
  131.4 8.0 %collective-permute-done.24.refs_7_.refs_1_.refs_14_ = bf16[3,48,1024]{2,1,0:T(8,128)(2,1)S(1)} collective-permute-done((bf16[3,48,1024]{2,1,0:T(8,128)(2,1)S(1)}, bf16[3,48,1024]{2,1,0:T(8,128)(2,1)S(1)}, u32[]{:S(2)}, u32[]{:S(2)}) %collective-permute-start.24) | collective-permute-done | bytes 294944 | tf_op jit(solution)/shard_map/ppermute | solution.py:80
  139.4 0.1 terms.5.refs_9_.refs_6_.refs_0_.refs_5_
  139.5 0.6 collective-permute-start.20
  140.1 2.3 %collective-permute-start.21 = (bf16[3,48,1024]{2,1,0:T(8,128)(2,1)S(1)}, bf16[3,48,1024]{2,1,0:T(8,128)(2,1)S(1)}, u32[]{:S(2)}, u32[]{:S(2)}) collective-permute-start(bf16[3,48,1024]{2,1,0:T(8,128)(2,1)S(1)} %terms.5.refs_9_.refs_6_.refs_0_.refs_5_), channel_id=1, source_target_pairs={{0,64},{32,224},{64,0},{96,160},{128,192},{160,96},{192,128},{224,... | collective-permute-start | bytes 884744 | tf_op jit(solution)/shard_map/ppermute | solution.py:74
  142.4 2.1 collective-permute-done.25.refs_8_.refs_2_.refs_15_
  144.5 4.6 %back_rows.3 = (bf16[192,896]{1,0:T(8,128)(2,1)S(1)}, bf16[192,896]{1,0:T(8,128)(2,1)S(1)}) custom-call(bf16[3,96,1024]{2,1,0:T(8,128)(2,1)S(1)} %terms.3.refs_2_.refs_0_.refs_9_, bf16[3,96,1024]{2,1,0:T(8,128)(2,1)S(1)} %collective-permute-done.17.refs_3_.refs_1_.refs_10_, bf16[3,96,1024]{2,1,0:T(8,128)(2,1)S(1)} %collective-permute-done.18.refs_4_.refs_2_.refs_11_, ...), custom_call_target="tpu_custom_call" | custom-call | flops 1 | bytes 1 | tf_op jit(solution)/shard_map/back_rows/pallas_call | solution.py:47
  149.1 2.1 collective-permute-start.26
  151.3 0.6 collective-permute-done.21.refs_8_.refs_2_.refs_7_
  151.8 3.1 %back_rows.4.refs_8_ = bf16[192,896]{1,0:T(8,128)(2,1)S(1)} custom-call(bf16[3,48,1024]{2,1,0:T(8,128)(2,1)S(1)} %terms.4.refs_5_.refs_6_.refs_0_.refs_13_, bf16[3,48,1024]{2,1,0:T(8,128)(2,1)S(1)} %collective-permute-done.24.refs_7_.refs_1_.refs_14_, bf16[3,48,1024]{2,1,0:T(8,128)(2,1)S(1)} %collective-permute-done.25.refs_8_.refs_2_.refs_15_, ...), custom_call_target="tpu_custom_call" | custom-call | flops 1 | bytes 1 | tf_op jit(solution)/shard_map/back_rows/pallas_call | solution.py:47
  155.0 2.2 %collective-permute-start.29 = (bf16[192,896]{1,0:T(8,128)(2,1)S(1)}, bf16[192,896]{1,0:T(8,128)(2,1)S(1)}, u32[]{:S(2)}, u32[]{:S(2)}) collective-permute-start(bf16[192,896]{1,0:T(8,128)(2,1)S(1)} %back_rows.4.refs_8_), channel_id=1, source_target_pairs={{0,16},{8,24},{16,0},{24,8},{1,17},{9,25},{17,1},{25,9},{2,18},{10... | collective-permute-start | bytes 1032200 | tf_op jit(solution)/shard_map/ppermute | solution.py:103
  157.2 7.1 %collective-permute-done.22.refs_3_.refs_8_ = bf16[3,48,1024]{2,1,0:T(8,128)(2,1)S(1)} collective-permute-done((bf16[3,48,1024]{2,1,0:T(8,128)(2,1)S(1)}, bf16[3,48,1024]{2,1,0:T(8,128)(2,1)S(1)}, u32[]{:S(2)}, u32[]{:S(2)}) %collective-permute-start.22) | collective-permute-done | bytes 294944 | tf_op jit(solution)/shard_map/ppermute | solution.py:74
  164.3 3.1 %back_rows.5.refs_2_.refs_6_ = bf16[192,896]{1,0:T(8,128)(2,1)S(1)} custom-call(bf16[3,48,1024]{2,1,0:T(8,128)(2,1)S(1)} %terms.5.refs_9_.refs_6_.refs_0_.refs_5_, bf16[3,48,1024]{2,1,0:T(8,128)(2,1)S(1)} %collective-permute-done.20.refs_7_.refs_1_.refs_6_, bf16[3,48,1024]{2,1,0:T(8,128)(2,1)S(1)} %collective-permute-done.21.refs_8_.refs_2_.refs_7_, ...), custom_call_target="tpu_custom_call" | custom-call | flops 1 | bytes 1 | tf_op jit(solution)/shard_map/back_rows/pallas_call | solution.py:47
  167.4 1.4 combine.1
  168.8 7.5 %collective-permute-start.30 = (bf16[448,896]{1,0:T(8,128)(2,1)S(1)}, bf16[448,896]{1,0:T(8,128)(2,1)S(1)}, u32[]{:S(2)}, u32[]{:S(2)}) collective-permute-start(bf16[448,896]{1,0:T(8,128)(2,1)S(1)} %get-tuple-element.71), channel_id=1, source_target_pairs={{0,32},{32,0},{1,33},{33,1},{2,34},{34,2},{3,35},{35,3},{4,36},{36... | collective-permute-start | bytes 2408456 | tf_op jit(solution)/shard_map/ppermute | solution.py:107
  176.3 1.9 collective-permute-done.30.refs_1_
  178.2 0.2 join.1
  178.4 2.4 %collective-permute-start.31 = (bf16[128,896]{1,0:T(8,128)(2,1)S(1)}, bf16[128,896]{1,0:T(8,128)(2,1)S(1)}, u32[]{:S(2)}, u32[]{:S(2)}) collective-permute-start(bf16[128,896]{1,0:T(8,128)(2,1)S(1)} %get-tuple-element.72.refs_17_), channel_id=1, source_target_pairs={{0,7},{1,0},{2,1},{3,2},{4,3},{5,4},{6,5},{7,6},{32,33},{33,34},{3... | collective-permute-start | bytes 688136 | tf_op jit(solution)/shard_map/ppermute | solution.py:88
  180.9 3.9 %collective-permute-start.32 = (bf16[128,896]{1,0:T(8,128)(2,1)S(1)}, bf16[128,896]{1,0:T(8,128)(2,1)S(1)}, u32[]{:S(2)}, u32[]{:S(2)}) collective-permute-start(bf16[128,896]{1,0:T(8,128)(2,1)S(1)} %get-tuple-element.73), channel_id=1, source_target_pairs={{0,6},{1,7},{2,0},{3,1},{4,2},{5,3},{6,4},{7,5},{32,34},{33,35},{3... | collective-permute-start | bytes 688136 | tf_op jit(solution)/shard_map/ppermute | solution.py:88
  184.8 3.7 %collective-permute-start.34 = (bf16[64,896]{1,0:T(8,128)(2,1)S(1)}, bf16[64,896]{1,0:T(8,128)(2,1)S(1)}, u32[]{:S(2)}, u32[]{:S(2)}) collective-permute-start(bf16[64,896]{1,0:T(8,128)(2,1)S(1)} %get-tuple-element.75), channel_id=1, source_target_pairs={{0,4},{1,5},{2,6},{3,7},{4,0},{5,1},{6,2},{7,3},{32,36},{33,37},{3... | collective-permute-start | bytes 344072 | tf_op jit(solution)/shard_map/ppermute | solution.py:88
  188.5 9.1 %weight_grads.1 = (f32[8,128]{1,0:T(8,128)S(1)}, bf16[2,896,512]{2,1,0:T(8,128)(2,1)}, bf16[2,896,512]{2,1,0:T(8,128)(2,1)}, bf16[2,512,896]{2,1,0:T(8,128)(2,1)}, bf16[2816,512]{1,0:T(8,128)(2,1)}) custom-call(s32[9]{0:T(128)S(1)} %copy-done.9, bf16[192,1792]{1,0:T(8,128)(2,1)S(1)} %get-tuple-element.49.refs_0_.refs_3_.refs_1_, ...), custom_call_target="tpu_custom_call" | custom-call | flops 1 | bytes 1 | tf_op jit(solution)/shard_map/weight_grads/pallas_call | solution.py:47
  197.5 0.3 collective-permute-done.34.refs_5_
  197.9 3.9 %collective-permute-done.33.refs_4_ = bf16[128,896]{1,0:T(8,128)(2,1)S(1)} collective-permute-done((bf16[128,896]{1,0:T(8,128)(2,1)S(1)}, bf16[128,896]{1,0:T(8,128)(2,1)S(1)}, u32[]{:S(2)}, u32[]{:S(2)}) %collective-permute-start.33) | collective-permute-done | bytes 229408 | tf_op jit(solution)/shard_map/ppermute | solution.py:88
  201.7 0.7 bring_home.1
  202.5 6.1 %collective-permute-start.36 = (bf16[2816,512]{1,0:T(8,128)(2,1)}, bf16[2816,512]{1,0:T(8,128)(2,1)S(1)}, u32[]{:S(2)}, u32[]{:S(2)}) collective-permute-start(bf16[2816,512]{1,0:T(8,128)(2,1)} %get-tuple-element.80), channel_id=1, source_target_pairs={{0,32},{32,0},{1,33},{33,1},{2,34},{34,2},{3,35},{35,3},{4,36},{36... | collective-permute-start | bytes 8650760 | tf_op jit(solution)/shard_map/ppermute | solution.py:107
  208.7 5.3 %collective-permute-done.35.refs_1_ = f32[128,896]{1,0:T(8,128)S(1)} collective-permute-done((f32[128,896]{1,0:T(8,128)S(1)}, f32[128,896]{1,0:T(8,128)S(1)}, u32[]{:S(2)}, u32[]{:S(2)}) %collective-permute-start.35) | collective-permute-done | bytes 458784 | tf_op jit(solution)/shard_map/ppermute | solution.py:107
  214.0 0.8 finish.1
  214.8 2.1 place_grads.1
  (54 shorter events, 0.9 us)
Async XLA Ops:
  5.9 42.7 %collective-permute-start.8 = (bf16[2816,512]{1,0:T(8,128)(2,1)}, bf16[2816,512]{1,0:T(8,128)(2,1)}, u32[]{:S(2)}, u32[]{:S(2)}) collective-permute-start(bf16[2816,512]{1,0:T(8,128)(2,1)} %get-tuple-element.51), channel_id=1, source_target_pairs={{0,32},{32,0},{1,33},{33,1},{2,34},{34,2},{3,35},{35,3},{4,36},{36... | collective-permute-start | bytes 8650760 | tf_op jit(solution)/shard_map/ppermute | solution.py:107
  6.7 35.3 %copy-start.6 = (bf16[128,1920]{1,0:T(8,128)(2,1)S(1)}, bf16[128,1920]{1,0:T(8,128)(2,1)}, u32[]{:S(2)}) copy-start(bf16[128,1920]{1,0:T(8,128)(2,1)} %get-tuple-element.46.refs_1_.refs_10_) | copy-start | bytes 1474564
  6.7 35.3 %copy-start.9 = (s32[9]{0:T(128)S(1)}, s32[9]{0:T(128)}, u32[]{:S(2)}) copy-start(s32[9]{0:T(128)} %stack.39.refs_0_.info) | copy-start | bytes 112
  6.7 16.1 %collective-permute-start.1 = (bf16[128,1920]{1,0:T(8,128)(2,1)}, bf16[128,1920]{1,0:T(8,128)(2,1)S(1)}, u32[]{:S(2)}, u32[]{:S(2)}) collective-permute-start(bf16[128,1920]{1,0:T(8,128)(2,1)} %get-tuple-element.46.refs_1_.refs_10_), channel_id=1, source_target_pairs={{0,2},{1,3},{2,4},{3,5},{4,6},{5,7},{6,0},{7,1},{32,38},{33,39},{3... | collective-permute-start | bytes 1474568 | tf_op jit(solution)/shard_map/ppermute | solution.py:88
  11.8 17.0 %collective-permute-start = (bf16[128,1920]{1,0:T(8,128)(2,1)}, bf16[128,1920]{1,0:T(8,128)(2,1)S(1)}, u32[]{:S(2)}, u32[]{:S(2)}) collective-permute-start(bf16[128,1920]{1,0:T(8,128)(2,1)} %get-tuple-element.46.refs_1_.refs_10_), channel_id=1, source_target_pairs={{0,1},{1,2},{2,3},{3,4},{4,5},{5,6},{6,7},{7,0},{32,39},{33,32},{3... | collective-permute-start | bytes 1474568 | tf_op jit(solution)/shard_map/ppermute | solution.py:88
  22.8 13.8 %collective-permute-start.3 = (bf16[128,1920]{1,0:T(8,128)(2,1)S(1)}, bf16[128,1920]{1,0:T(8,128)(2,1)S(1)}, u32[]{:S(2)}, u32[]{:S(2)}) collective-permute-start(bf16[128,1920]{1,0:T(8,128)(2,1)S(1)} %collective-permute-done.1.refs_3_), channel_id=1, source_target_pairs={{0,2},{2,4},{4,6},{6,0},{33,39},{35,33},{37,35},{39,37},{8,10},{10... | collective-permute-start | bytes 1474568 | tf_op jit(solution)/shard_map/ppermute | solution.py:94
  28.7 11.1 %collective-permute-start.2 = (bf16[128,1920]{1,0:T(8,128)(2,1)S(1)}, bf16[128,1920]{1,0:T(8,128)(2,1)S(1)}, u32[]{:S(2)}, u32[]{:S(2)}) collective-permute-start(bf16[128,1920]{1,0:T(8,128)(2,1)S(1)} %collective-permute-done.1.refs_3_), channel_id=1, source_target_pairs={{0,1},{1,2},{2,3},{3,4},{4,5},{5,6},{6,7},{7,0},{32,39},{33,32},{3... | collective-permute-start | bytes 1474568 | tf_op jit(solution)/shard_map/ppermute | solution.py:88
  28.8 0.8 copy-start.7
  33.6 15.1 %copy-start = (bf16[2816,512]{1,0:T(8,128)(2,1)S(1)}, bf16[2816,512]{1,0:T(8,128)(2,1)}, u32[]{:S(2)}) copy-start(bf16[2816,512]{1,0:T(8,128)(2,1)} %get-tuple-element.50.refs_1_.refs_2_.refs_4_) | copy-start | bytes 8650756
  33.6 6.9 %collective-permute-start.5 = (bf16[128,1920]{1,0:T(8,128)(2,1)}, bf16[128,1920]{1,0:T(8,128)(2,1)S(1)}, u32[]{:S(2)}, u32[]{:S(2)}) collective-permute-start(bf16[128,1920]{1,0:T(8,128)(2,1)} %get-tuple-element.47.refs_2_), channel_id=1, source_target_pairs={{0,32},{32,0},{1,33},{33,1},{2,34},{34,2},{3,35},{35,3},{4,36},{36... | collective-permute-start | bytes 1474568 | tf_op jit(solution)/shard_map/ppermute | solution.py:107
  36.5 4.0 %collective-permute-start.6 = (bf16[128,1920]{1,0:T(8,128)(2,1)S(1)}, bf16[128,1920]{1,0:T(8,128)(2,1)S(1)}, u32[]{:S(2)}, u32[]{:S(2)}) collective-permute-start(bf16[128,1920]{1,0:T(8,128)(2,1)S(1)} %collective-permute-done.1.refs_3_), channel_id=1, source_target_pairs={{0,32},{32,0},{1,33},{33,1},{2,34},{34,2},{3,35},{35,3},{4,36},{36... | collective-permute-start | bytes 1474568 | tf_op jit(solution)/shard_map/ppermute | solution.py:107
  36.6 3.9 %collective-permute-start.4 = (bf16[128,1920]{1,0:T(8,128)(2,1)S(1)}, bf16[128,1920]{1,0:T(8,128)(2,1)S(1)}, u32[]{:S(2)}, u32[]{:S(2)}) collective-permute-start(bf16[128,1920]{1,0:T(8,128)(2,1)S(1)} %collective-permute-done.3.refs_5_), channel_id=1, source_target_pairs={{0,32},{33,1},{2,34},{35,3},{4,36},{37,5},{6,38},{39,7},{8,40},{41... | collective-permute-start | bytes 1474568 | tf_op jit(solution)/shard_map/ppermute | solution.py:99
  39.7 2.3 %collective-permute-start.7 = (bf16[128,1920]{1,0:T(8,128)(2,1)S(1)}, bf16[128,1920]{1,0:T(8,128)(2,1)S(1)}, u32[]{:S(2)}, u32[]{:S(2)}) collective-permute-start(bf16[128,1920]{1,0:T(8,128)(2,1)S(1)} %collective-permute-done.2.refs_4_), channel_id=1, source_target_pairs={{0,32},{32,0},{1,33},{33,1},{2,34},{34,2},{3,35},{35,3},{4,36},{36... | collective-permute-start | bytes 1474568 | tf_op jit(solution)/shard_map/ppermute | solution.py:107
  42.0 1.0 copy-start.8
  46.0 17.9 %collective-permute-start.11 = (bf16[192,1792]{1,0:T(8,128)(2,1)S(1)}, bf16[192,1792]{1,0:T(8,128)(2,1)S(1)}, u32[]{:S(2)}, u32[]{:S(2)}) collective-permute-start(bf16[192,1792]{1,0:T(8,128)(2,1)S(1)} %get-tuple-element.56), channel_id=1, source_target_pairs={{0,8},{8,16},{16,24},{24,0},{1,9},{9,17},{17,25},{25,1},{2,10},{10... | collective-permute-start | bytes 2064392 | tf_op jit(solution)/shard_map/ppermute | solution.py:103
  47.2 16.7 %collective-permute-start.12 = (bf16[192,1792]{1,0:T(8,128)(2,1)}, bf16[192,1792]{1,0:T(8,128)(2,1)S(1)}, u32[]{:S(2)}, u32[]{:S(2)}) collective-permute-start(bf16[192,1792]{1,0:T(8,128)(2,1)} %get-tuple-element.57), channel_id=1, source_target_pairs={{0,24},{8,0},{16,8},{24,16},{1,25},{9,1},{17,9},{25,17},{2,26},{10... | collective-permute-start | bytes 2064392 | tf_op jit(solution)/shard_map/ppermute | solution.py:103
  52.1 10.4 %collective-permute-start.9 = (bf16[3,96,1024]{2,1,0:T(8,128)(2,1)S(1)}, bf16[3,96,1024]{2,1,0:T(8,128)(2,1)S(1)}, u32[]{:S(2)}, u32[]{:S(2)}) collective-permute-start(bf16[3,96,1024]{2,1,0:T(8,128)(2,1)S(1)} %get-tuple-element.53), channel_id=1, source_target_pairs={{0,64},{32,224},{64,0},{96,160},{128,192},{160,96},{192,128},{224,... | collective-permute-start | bytes 1769480 | tf_op jit(solution)/shard_map/ppermute | solution.py:74
  63.8 5.8 %copy-start.4 = (bf16[192,1792]{1,0:T(8,128)(2,1)}, bf16[192,1792]{1,0:T(8,128)(2,1)S(1)}, u32[]{:S(2)}) copy-start(bf16[192,1792]{1,0:T(8,128)(2,1)S(1)} %collective-permute-done.11.refs_0_.refs_2_) | copy-start | bytes 2064388
  63.8 5.8 %copy-start.5 = (bf16[192,1792]{1,0:T(8,128)(2,1)}, bf16[192,1792]{1,0:T(8,128)(2,1)S(1)}, u32[]{:S(2)}) copy-start(bf16[192,1792]{1,0:T(8,128)(2,1)S(1)} %collective-permute-done.12.refs_1_.refs_4_) | copy-start | bytes 2064388
  63.8 8.7 %copy-start.10 = (bf16[192,1792]{1,0:T(8,128)(2,1)S(1)}, bf16[192,1792]{1,0:T(8,128)(2,1)}, u32[]{:S(2)}) copy-start(bf16[192,1792]{1,0:T(8,128)(2,1)} %get-tuple-element.60) | copy-start | bytes 2064388
  69.7 25.9 %copy-start.2 = (f32[3,192,1024]{2,1,0:T(8,128)}, f32[3,192,1024]{2,1,0:T(8,128)S(1)}, u32[]{:S(2)}) copy-start(f32[3,192,1024]{2,1,0:T(8,128)S(1)} %get-tuple-element.58.refs_4_.refs_0_) | copy-start | bytes 7077892
  69.7 26.0 %collective-permute-start.13 = (bf16[3,192,1024]{2,1,0:T(8,128)(2,1)S(1)}, bf16[3,192,1024]{2,1,0:T(8,128)(2,1)S(1)}, u32[]{:S(2)}, u32[]{:S(2)}) collective-permute-start(bf16[3,192,1024]{2,1,0:T(8,128)(2,1)S(1)} %get-tuple-element.59), channel_id=1, source_target_pairs={{0,64},{32,224},{64,0},{96,160},{128,192},{160,96},{192,128},{224,... | collective-permute-start | bytes 3538952 | tf_op jit(solution)/shard_map/ppermute | solution.py:74
  72.5 18.5 %collective-permute-start.14 = (bf16[192,1792]{1,0:T(8,128)(2,1)S(1)}, bf16[192,1792]{1,0:T(8,128)(2,1)S(1)}, u32[]{:S(2)}, u32[]{:S(2)}) collective-permute-start(bf16[192,1792]{1,0:T(8,128)(2,1)S(1)} %copy-done.10), channel_id=1, source_target_pairs={{0,16},{8,24},{16,0},{24,8},{1,17},{9,25},{17,1},{25,9},{2,18},{10... | collective-permute-start | bytes 2064392 | tf_op jit(solution)/shard_map/ppermute | solution.py:103
  74.6 16.4 %collective-permute-start.10 = (bf16[3,48,1024]{2,1,0:T(8,128)(2,1)S(1)}, bf16[3,48,1024]{2,1,0:T(8,128)(2,1)S(1)}, u32[]{:S(2)}, u32[]{:S(2)}) collective-permute-start(bf16[3,48,1024]{2,1,0:T(8,128)(2,1)S(1)} %get-tuple-element.55), channel_id=1, source_target_pairs={{0,192},{32,96},{64,128},{96,32},{128,64},{160,224},{192,0},{224,1... | collective-permute-start | bytes 884744 | tf_op jit(solution)/shard_map/ppermute | solution.py:80
  91.0 4.5 %copy-start.3 = (bf16[192,1792]{1,0:T(8,128)(2,1)}, bf16[192,1792]{1,0:T(8,128)(2,1)S(1)}, u32[]{:S(2)}) copy-start(bf16[192,1792]{1,0:T(8,128)(2,1)S(1)} %collective-permute-done.14.refs_0_.refs_3_) | copy-start | bytes 2064388
  95.6 13.2 %collective-permute-start.16 = (bf16[3,96,1024]{2,1,0:T(8,128)(2,1)S(1)}, bf16[3,96,1024]{2,1,0:T(8,128)(2,1)S(1)}, u32[]{:S(2)}, u32[]{:S(2)}) collective-permute-start(bf16[3,96,1024]{2,1,0:T(8,128)(2,1)S(1)} %get-tuple-element.64), channel_id=1, source_target_pairs={{0,64},{32,224},{64,0},{96,160},{128,192},{160,96},{192,128},{224,... | collective-permute-start | bytes 1769480 | tf_op jit(solution)/shard_map/ppermute | solution.py:74
  97.6 14.7 %collective-permute-start.15 = (bf16[3,96,1024]{2,1,0:T(8,128)(2,1)S(1)}, bf16[3,96,1024]{2,1,0:T(8,128)(2,1)S(1)}, u32[]{:S(2)}, u32[]{:S(2)}) collective-permute-start(bf16[3,96,1024]{2,1,0:T(8,128)(2,1)S(1)} %get-tuple-element.63), channel_id=1, source_target_pairs={{0,192},{32,96},{64,128},{96,32},{128,64},{160,224},{192,0},{224,1... | collective-permute-start | bytes 1769480 | tf_op jit(solution)/shard_map/ppermute | solution.py:80
  112.5 11.3 %collective-permute-start.17 = (bf16[3,96,1024]{2,1,0:T(8,128)(2,1)S(1)}, bf16[3,96,1024]{2,1,0:T(8,128)(2,1)S(1)}, u32[]{:S(2)}, u32[]{:S(2)}) collective-permute-start(bf16[3,96,1024]{2,1,0:T(8,128)(2,1)S(1)} %terms.3.refs_2_.refs_0_.refs_9_), channel_id=1, source_target_pairs={{0,192},{32,96},{64,128},{96,32},{128,64},{160,224},{192,0},{224,1... | collective-permute-start | bytes 1769480 | tf_op jit(solution)/shard_map/ppermute | solution.py:80
  112.6 17.5 %collective-permute-start.19 = (bf16[3,48,1024]{2,1,0:T(8,128)(2,1)S(1)}, bf16[3,48,1024]{2,1,0:T(8,128)(2,1)S(1)}, u32[]{:S(2)}, u32[]{:S(2)}) collective-permute-start(bf16[3,48,1024]{2,1,0:T(8,128)(2,1)S(1)} %get-tuple-element.66), channel_id=1, source_target_pairs={{0,192},{32,96},{64,128},{96,32},{128,64},{160,224},{192,0},{224,1... | collective-permute-start | bytes 884744 | tf_op jit(solution)/shard_map/ppermute | solution.py:80
  114.1 25.3 %collective-permute-start.18 = (bf16[3,96,1024]{2,1,0:T(8,128)(2,1)S(1)}, bf16[3,96,1024]{2,1,0:T(8,128)(2,1)S(1)}, u32[]{:S(2)}, u32[]{:S(2)}) collective-permute-start(bf16[3,96,1024]{2,1,0:T(8,128)(2,1)S(1)} %terms.3.refs_2_.refs_0_.refs_9_), channel_id=1, source_target_pairs={{0,64},{32,224},{64,0},{96,160},{128,192},{160,96},{192,128},{224,... | collective-permute-start | bytes 1769480 | tf_op jit(solution)/shard_map/ppermute | solution.py:74
  123.8 20.7 %collective-permute-start.23 = (bf16[3,96,1024]{2,1,0:T(8,128)(2,1)S(1)}, bf16[3,96,1024]{2,1,0:T(8,128)(2,1)S(1)}, u32[]{:S(2)}, u32[]{:S(2)}) collective-permute-start(bf16[3,96,1024]{2,1,0:T(8,128)(2,1)S(1)} %collective-permute-done.17.refs_3_.refs_1_.refs_10_), channel_id=1, source_target_pairs={{0,64},{32,224},{64,0},{96,160},{128,192},{160,96},{192,128},{224,... | collective-permute-start | bytes 1769480 | tf_op jit(solution)/shard_map/ppermute | solution.py:74
  130.3 9.1 %collective-permute-start.24 = (bf16[3,48,1024]{2,1,0:T(8,128)(2,1)S(1)}, bf16[3,48,1024]{2,1,0:T(8,128)(2,1)S(1)}, u32[]{:S(2)}, u32[]{:S(2)}) collective-permute-start(bf16[3,48,1024]{2,1,0:T(8,128)(2,1)S(1)} %terms.4.refs_5_.refs_6_.refs_0_.refs_13_), channel_id=1, source_target_pairs={{0,192},{32,96},{64,128},{96,32},{128,64},{160,224},{192,0},{224,1... | collective-permute-start | bytes 884744 | tf_op jit(solution)/shard_map/ppermute | solution.py:80
  130.6 13.8 %collective-permute-start.25 = (bf16[3,48,1024]{2,1,0:T(8,128)(2,1)S(1)}, bf16[3,48,1024]{2,1,0:T(8,128)(2,1)S(1)}, u32[]{:S(2)}, u32[]{:S(2)}) collective-permute-start(bf16[3,48,1024]{2,1,0:T(8,128)(2,1)S(1)} %terms.4.refs_5_.refs_6_.refs_0_.refs_13_), channel_id=1, source_target_pairs={{0,64},{32,224},{64,0},{96,160},{128,192},{160,96},{192,128},{224,... | collective-permute-start | bytes 884744 | tf_op jit(solution)/shard_map/ppermute | solution.py:74
  139.4 11.9 %collective-permute-start.28 = (bf16[3,48,1024]{2,1,0:T(8,128)(2,1)S(1)}, bf16[3,48,1024]{2,1,0:T(8,128)(2,1)S(1)}, u32[]{:S(2)}, u32[]{:S(2)}) collective-permute-start(bf16[3,48,1024]{2,1,0:T(8,128)(2,1)S(1)} %collective-permute-done.24.refs_7_.refs_1_.refs_14_), channel_id=1, source_target_pairs={{0,64},{32,224},{64,0},{96,160},{128,192},{160,96},{192,128},{224,... | collective-permute-start | bytes 884744 | tf_op jit(solution)/shard_map/ppermute | solution.py:74
  139.5 11.8 %collective-permute-start.20 = (bf16[3,48,1024]{2,1,0:T(8,128)(2,1)S(1)}, bf16[3,48,1024]{2,1,0:T(8,128)(2,1)S(1)}, u32[]{:S(2)}, u32[]{:S(2)}) collective-permute-start(bf16[3,48,1024]{2,1,0:T(8,128)(2,1)S(1)} %terms.5.refs_9_.refs_6_.refs_0_.refs_5_), channel_id=1, source_target_pairs={{0,192},{32,96},{64,128},{96,32},{128,64},{160,224},{192,0},{224,1... | collective-permute-start | bytes 884744 | tf_op jit(solution)/shard_map/ppermute | solution.py:80
  140.1 11.7 %collective-permute-start.21 = (bf16[3,48,1024]{2,1,0:T(8,128)(2,1)S(1)}, bf16[3,48,1024]{2,1,0:T(8,128)(2,1)S(1)}, u32[]{:S(2)}, u32[]{:S(2)}) collective-permute-start(bf16[3,48,1024]{2,1,0:T(8,128)(2,1)S(1)} %terms.5.refs_9_.refs_6_.refs_0_.refs_5_), channel_id=1, source_target_pairs={{0,64},{32,224},{64,0},{96,160},{128,192},{160,96},{192,128},{224,... | collective-permute-start | bytes 884744 | tf_op jit(solution)/shard_map/ppermute | solution.py:74
  144.5 7.4 %copy-start.1 = (bf16[2816,512]{1,0:T(8,128)(2,1)S(1)}, bf16[2816,512]{1,0:T(8,128)(2,1)}, u32[]{:S(2)}) copy-start(bf16[2816,512]{1,0:T(8,128)(2,1)} %get-tuple-element.50.refs_1_.refs_2_.refs_4_) | copy-start | bytes 8650756
  149.1 15.2 %collective-permute-start.26 = (bf16[192,896]{1,0:T(8,128)(2,1)S(1)}, bf16[192,896]{1,0:T(8,128)(2,1)S(1)}, u32[]{:S(2)}, u32[]{:S(2)}) collective-permute-start(bf16[192,896]{1,0:T(8,128)(2,1)S(1)} %get-tuple-element.67.refs_9_), channel_id=1, source_target_pairs={{0,24},{8,0},{16,8},{24,16},{1,25},{9,1},{17,9},{25,17},{2,26},{10... | collective-permute-start | bytes 1032200 | tf_op jit(solution)/shard_map/ppermute | solution.py:103
  151.3 13.0 %collective-permute-start.27 = (bf16[192,896]{1,0:T(8,128)(2,1)S(1)}, bf16[192,896]{1,0:T(8,128)(2,1)S(1)}, u32[]{:S(2)}, u32[]{:S(2)}) collective-permute-start(bf16[192,896]{1,0:T(8,128)(2,1)S(1)} %get-tuple-element.68), channel_id=1, source_target_pairs={{0,8},{8,16},{16,24},{24,0},{1,9},{9,17},{17,25},{25,1},{2,10},{10... | collective-permute-start | bytes 1032200 | tf_op jit(solution)/shard_map/ppermute | solution.py:103
  155.0 12.5 %collective-permute-start.29 = (bf16[192,896]{1,0:T(8,128)(2,1)S(1)}, bf16[192,896]{1,0:T(8,128)(2,1)S(1)}, u32[]{:S(2)}, u32[]{:S(2)}) collective-permute-start(bf16[192,896]{1,0:T(8,128)(2,1)S(1)} %back_rows.4.refs_8_), channel_id=1, source_target_pairs={{0,16},{8,24},{16,0},{24,8},{1,17},{9,25},{17,1},{25,9},{2,18},{10... | collective-permute-start | bytes 1032200 | tf_op jit(solution)/shard_map/ppermute | solution.py:103
  157.2 7.1 %collective-permute-start.22 = (bf16[3,48,1024]{2,1,0:T(8,128)(2,1)S(1)}, bf16[3,48,1024]{2,1,0:T(8,128)(2,1)S(1)}, u32[]{:S(2)}, u32[]{:S(2)}) collective-permute-start(bf16[3,48,1024]{2,1,0:T(8,128)(2,1)S(1)} %collective-permute-done.20.refs_7_.refs_1_.refs_6_), channel_id=1, source_target_pairs={{0,64},{32,224},{64,0},{96,160},{128,192},{160,96},{192,128},{224,... | collective-permute-start | bytes 884744 | tf_op jit(solution)/shard_map/ppermute | solution.py:74
  168.8 9.4 %collective-permute-start.30 = (bf16[448,896]{1,0:T(8,128)(2,1)S(1)}, bf16[448,896]{1,0:T(8,128)(2,1)S(1)}, u32[]{:S(2)}, u32[]{:S(2)}) collective-permute-start(bf16[448,896]{1,0:T(8,128)(2,1)S(1)} %get-tuple-element.71), channel_id=1, source_target_pairs={{0,32},{32,0},{1,33},{33,1},{2,34},{34,2},{3,35},{35,3},{4,36},{36... | collective-permute-start | bytes 2408456 | tf_op jit(solution)/shard_map/ppermute | solution.py:107
  178.4 19.4 %collective-permute-start.31 = (bf16[128,896]{1,0:T(8,128)(2,1)S(1)}, bf16[128,896]{1,0:T(8,128)(2,1)S(1)}, u32[]{:S(2)}, u32[]{:S(2)}) collective-permute-start(bf16[128,896]{1,0:T(8,128)(2,1)S(1)} %get-tuple-element.72.refs_17_), channel_id=1, source_target_pairs={{0,7},{1,0},{2,1},{3,2},{4,3},{5,4},{6,5},{7,6},{32,33},{33,34},{3... | collective-permute-start | bytes 688136 | tf_op jit(solution)/shard_map/ppermute | solution.py:88
  180.9 17.0 %collective-permute-start.32 = (bf16[128,896]{1,0:T(8,128)(2,1)S(1)}, bf16[128,896]{1,0:T(8,128)(2,1)S(1)}, u32[]{:S(2)}, u32[]{:S(2)}) collective-permute-start(bf16[128,896]{1,0:T(8,128)(2,1)S(1)} %get-tuple-element.73), channel_id=1, source_target_pairs={{0,6},{1,7},{2,0},{3,1},{4,2},{5,3},{6,4},{7,5},{32,34},{33,35},{3... | collective-permute-start | bytes 688136 | tf_op jit(solution)/shard_map/ppermute | solution.py:88
  184.8 17.0 %collective-permute-start.33 = (bf16[128,896]{1,0:T(8,128)(2,1)S(1)}, bf16[128,896]{1,0:T(8,128)(2,1)S(1)}, u32[]{:S(2)}, u32[]{:S(2)}) collective-permute-start(bf16[128,896]{1,0:T(8,128)(2,1)S(1)} %get-tuple-element.74), channel_id=1, source_target_pairs={{0,5},{1,6},{2,7},{3,0},{4,1},{5,2},{6,3},{7,4},{32,35},{33,36},{3... | collective-permute-start | bytes 688136 | tf_op jit(solution)/shard_map/ppermute | solution.py:88
  184.8 13.1 %collective-permute-start.34 = (bf16[64,896]{1,0:T(8,128)(2,1)S(1)}, bf16[64,896]{1,0:T(8,128)(2,1)S(1)}, u32[]{:S(2)}, u32[]{:S(2)}) collective-permute-start(bf16[64,896]{1,0:T(8,128)(2,1)S(1)} %get-tuple-element.75), channel_id=1, source_target_pairs={{0,4},{1,5},{2,6},{3,7},{4,0},{5,1},{6,2},{7,3},{32,36},{33,37},{3... | collective-permute-start | bytes 344072 | tf_op jit(solution)/shard_map/ppermute | solution.py:88
  202.5 12.3 %collective-permute-start.36 = (bf16[2816,512]{1,0:T(8,128)(2,1)}, bf16[2816,512]{1,0:T(8,128)(2,1)S(1)}, u32[]{:S(2)}, u32[]{:S(2)}) collective-permute-start(bf16[2816,512]{1,0:T(8,128)(2,1)} %get-tuple-element.80), channel_id=1, source_target_pairs={{0,32},{32,0},{1,33},{33,1},{2,34},{34,2},{3,35},{35,3},{4,36},{36... | collective-permute-start | bytes 8650760 | tf_op jit(solution)/shard_map/ppermute | solution.py:107
  208.6 5.4 %collective-permute-start.35 = (f32[128,896]{1,0:T(8,128)S(1)}, f32[128,896]{1,0:T(8,128)S(1)}, u32[]{:S(2)}, u32[]{:S(2)}) collective-permute-start(f32[128,896]{1,0:T(8,128)S(1)} %get-tuple-element.78.refs_0_.refs_2_), channel_id=1, source_target_pairs={{0,32},{32,0},{1,33},{33,1},{2,34},{34,2},{3,35},{35,3},{4,36},{36... | collective-permute-start | bytes 1376264 | tf_op jit(solution)/shard_map/ppermute | solution.py:107
where the time goes:
time: 217 us
  waiting for transfers between devices  97.4 us (45%)
  starting transfers between devices  63 us (29%)
  Pallas kernels  52.9 us (24%)
  local copies, waits for them, and re-layouts  2.52 us (1%)
    pallas_call x20, Pallas kernels, __call__(): pl.pallas_call(run, out_shape=[jax.ShapeDtypeStruct(s, t) for s, t in out...  50.8 us
    ppermute x9, waiting for transfers between devices, to_first(): lax.ppermute(v, ('dp', 'seq'), [(y * 2 + s, first(y, s) * 2 + s) for y in...  28.4 us
    ppermute x6, waiting for transfers between devices, to_second(): lax.ppermute(v, ('dp', 'seq'), [(y * 2 + s, second(y, s) * 2 + s) for y i...  27.3 us
    ppermute x7, starting transfers between devices, swap(): return lax.ppermute(v, 'seq', [(0, 1), (1, 0)])  18.2 us
    ppermute x6, waiting for transfers between devices, along_x(): return lax.ppermute(v, 'ex', [(x, (x + far) % NX) for x in range(NX)])  17.7 us
    ppermute x7, starting transfers between devices, along_z(): return lax.ppermute(v, ('seq', 'ez'), pairs)  16 us
    ppermute x7, waiting for transfers between devices, along_z(): return lax.ppermute(v, ('seq', 'ez'), pairs)  15.1 us
    ppermute x6, starting transfers between devices, along_x(): return lax.ppermute(v, 'ex', [(x, (x + far) % NX) for x in range(NX)])  9.16 us
  transfers between devices with their start and end apart: 37, of which 18 were waited for; matrix products, arithmetic and copies ran while one was open for 0% of the time, Pallas kernels for 17%

commit v1 on v0

--- a/solution.py
+++ b/solution.py
@@ -36,7 +36,7 @@
         self.last = None
 
     def __call__(
-        self, body, outs, ins, scratch=(), name=None, after=(), hand=(), hbm=False, limit=48, free=False
+        self, body, outs, ins, scratch=(), name=None, after=(), hand=(), hbm=False, limit=24, free=False
     ):
         waits = list(after) + ([] if free or self.last is None else [self.last])
         n, k, h, m = len(ins), len(waits), len(hand), len(outs)
@@ -468,10 +468,10 @@
     reduce(1)
     reduce(2)
     spread(1)
+    spread(0, *parts[1][1:3])
     spread(2)
-    spread(0, *parts[1][:3])
-    back(1, *parts[2][:3])
-    back(2, *parts[0][:3])
+    back(1, *parts[2][1:3])
+    back(2, *parts[0][1:3])
     back(0, returned[1], returned[3])
 
     home, mine, theirs = queue(
@@ -495,6 +495,7 @@
         (info, *messages, *[a for part in parts for a in part]),
         [((4 * MR, 2 * DC), BF), ((3, 4 * MR, 1024), BF)],
         name="weight_grads",
+        limit=48,
     )
     total, send = queue(
         bring_home, [((TB, DC), F32)], (info, home, *homed), hand=(send,), name="bring_home"

time: 217 us -> 206 us (0.949)
  Pallas kernels: 52.9 us -> 36.4 us
  waiting for transfers between devices: 97.4 us -> 101 us
    pallas_call x20, Pallas kernels: 50.8 us -> 34.3 us  [__call__(): pl.pallas_call(run, out_shape=[jax.ShapeDtypeStruct(s, t) for s, t in out...]
    ppermute x9, waiting for transfers between devices: 28.4 us -> 37.5 us  [to_first(): lax.ppermute(v, ('dp', 'seq'), [(y * 2 + s, first(y, s) * 2 + s) for y in...]
    ppermute x6, waiting for transfers between devices: 27.3 us -> 19.3 us  [to_second(): lax.ppermute(v, ('dp', 'seq'), [(y * 2 + s, second(y, s) * 2 + s) for y i...]
    ppermute x9, starting transfers between devices: 8.78 us -> 15.4 us  [to_first(): lax.ppermute(v, ('dp', 'seq'), [(y * 2 + s, first(y, s) * 2 + s) for y in...]
    ppermute x7, starting transfers between devices: 18.2 us -> 15.4 us  [swap(): return lax.ppermute(v, 'seq', [(0, 1), (1, 0)])]
    ppermute x6, waiting for transfers between devices: 17.7 us -> 20 us  [along_x(): return lax.ppermute(v, 'ex', [(x, (x + far) % NX) for x in range(NX)])]
  transfers between devices with their start and end apart: 37 -> 37, of which waited for: 18 -> 21; matrix products, arithmetic and copies ran while one was open for 0% -> 0% of each run, Pallas kernels for 17% -> 12%
where the time goes in v1:
time: 206 us; the launch traced here: 205 us
  waiting for transfers between devices  101 us (49%)
  starting transfers between devices  64.1 us (31%)
  Pallas kernels  36.4 us (18%)
  local copies, waits for them, and re-layouts  2.4 us (1%)
    ppermute x9, waiting for transfers between devices, to_first(): lax.ppermute(v, ('dp', 'seq'), [(y * 2 + s, first(y, s) * 2 + s) for y in...  37.5 us
    pallas_call x20, Pallas kernels, __call__(): pl.pallas_call(run, out_shape=[jax.ShapeDtypeStruct(s, t) for s, t in out...  34.3 us
    ppermute x6, waiting for transfers between devices, along_x(): return lax.ppermute(v, 'ex', [(x, (x + far) % NX) for x in range(NX)])  20 us
    ppermute x6, waiting for transfers between devices, to_second(): lax.ppermute(v, ('dp', 'seq'), [(y * 2 + s, second(y, s) * 2 + s) for y i...  19.3 us
    ppermute x7, starting transfers between devices, along_z(): return lax.ppermute(v, ('seq', 'ez'), pairs)  16.1 us
    ppermute x7, waiting for transfers between devices, along_z(): return lax.ppermute(v, ('seq', 'ez'), pairs)  15.5 us
    ppermute x9, starting transfers between devices, to_first(): lax.ppermute(v, ('dp', 'seq'), [(y * 2 + s, first(y, s) * 2 + s) for y in...  15.4 us
    ppermute x7, starting transfers between devices, swap(): return lax.ppermute(v, 'seq', [(0, 1), (1, 0)])  15.4 us
  transfers between devices with their start and end apart: 37, of which 21 were waited for; matrix products, arithmetic and copies ran while one was open for 0% of the time, Pallas kernels for 12%

profile of v1, /device:TPU:33, one launch (start us, length us, event | category | flops | bytes accessed | tf_op | source)
XLA Modules:
  0.0 205.3 jit_solution(8492775745012784334)
XLA Ops:
  0.7 0.6 stack.39.refs_0_.info
  1.3 4.4 %pack.1 = (bf16[128,1920]{1,0:T(8,128)(2,1)}, bf16[2816,512]{1,0:T(8,128)(2,1)}) custom-call(s32[9]{0:T(128)} %stack.39.refs_0_.info, bf16[128,896]{1,0:T(8,128)(2,1)} %refs_1_.2, bf16[128,896]{1,0:T(8,128)(2,1)} %refs_2_.2, s32[8,128]{1,0:T(8,128)} %bitcast.11, f32[8,128]{1,0:T(8,128)} %bitcast.12, bf16[2,896,512]{2,1,0:T(8,128)(2,1)} %refs_1_.3, ...), custom_call_target="tpu_custom_call" | custom-call | flops 1 | bytes 1 | tf_op jit(solution)/shard_map/pack/pallas_call | solution.py:47
  5.7 0.8 collective-permute-start.8
  6.5 5.1 %collective-permute-start.1 = (bf16[128,1920]{1,0:T(8,128)(2,1)}, bf16[128,1920]{1,0:T(8,128)(2,1)}, u32[]{:S(2)}, u32[]{:S(2)}) collective-permute-start(bf16[128,1920]{1,0:T(8,128)(2,1)} %get-tuple-element.46.refs_1_.refs_10_), channel_id=1, source_target_pairs={{0,2},{1,3},{2,4},{3,5},{4,6},{5,7},{6,0},{7,1},{32,38},{33,39},{3... | collective-permute-start | bytes 1474568 | tf_op jit(solution)/shard_map/ppermute | solution.py:88
  11.6 0.7 collective-permute-start
  12.4 10.3 %collective-permute-done.1.refs_3_ = bf16[128,1920]{1,0:T(8,128)(2,1)} collective-permute-done((bf16[128,1920]{1,0:T(8,128)(2,1)}, bf16[128,1920]{1,0:T(8,128)(2,1)}, u32[]{:S(2)}, u32[]{:S(2)}) %collective-permute-start.1) | collective-permute-done | bytes 491552 | tf_op jit(solution)/shard_map/ppermute | solution.py:88
  22.6 6.0 %collective-permute-start.3 = (bf16[128,1920]{1,0:T(8,128)(2,1)}, bf16[128,1920]{1,0:T(8,128)(2,1)}, u32[]{:S(2)}, u32[]{:S(2)}) collective-permute-start(bf16[128,1920]{1,0:T(8,128)(2,1)} %collective-permute-done.1.refs_3_), channel_id=1, source_target_pairs={{0,2},{2,4},{4,6},{6,0},{33,39},{35,33},{37,35},{39,37},{8,10},{10... | collective-permute-start | bytes 1474568 | tf_op jit(solution)/shard_map/ppermute | solution.py:94
  28.7 0.8 copy-done.5
  29.5 4.0 %pack_own.1 = (bf16[2816,512]{1,0:T(8,128)(2,1)}, bf16[128,1920]{1,0:T(8,128)(2,1)}) custom-call(s32[9]{0:T(128)} %stack.39.refs_0_.info, bf16[2,896,512]{2,1,0:T(8,128)(2,1)} %refs_1_.3, bf16[2,896,512]{2,1,0:T(8,128)(2,1)} %refs_2_.3, bf16[2,512,896]{2,1,0:T(8,128)(2,1)} %refs_3_.1, bf16[128,1920]{1,0:T(8,128)(2,1)} %copy-done.5), custom_call_target="tpu_custom_call", output_to_operand_aliasing={{1}: (4, {})} | custom-call | flops 1 | bytes 1 | tf_op jit(solution)/shard_map/pack_own/pallas_call | solution.py:47
  33.5 2.9 %collective-permute-start.5 = (bf16[128,1920]{1,0:T(8,128)(2,1)}, bf16[128,1920]{1,0:T(8,128)(2,1)S(1)}, u32[]{:S(2)}, u32[]{:S(2)}) collective-permute-start(bf16[128,1920]{1,0:T(8,128)(2,1)} %get-tuple-element.47.refs_2_), channel_id=1, source_target_pairs={{0,32},{32,0},{1,33},{33,1},{2,34},{34,2},{3,35},{35,3},{4,36},{36... | collective-permute-start | bytes 1474568 | tf_op jit(solution)/shard_map/ppermute | solution.py:107
  36.5 2.5 %collective-permute-start.4 = (bf16[128,1920]{1,0:T(8,128)(2,1)}, bf16[128,1920]{1,0:T(8,128)(2,1)S(1)}, u32[]{:S(2)}, u32[]{:S(2)}) collective-permute-start(bf16[128,1920]{1,0:T(8,128)(2,1)} %collective-permute-done.3.refs_5_), channel_id=1, source_target_pairs={{0,32},{33,1},{2,34},{35,3},{4,36},{37,5},{6,38},{39,7},{8,40},{41... | collective-permute-start | bytes 1474568 | tf_op jit(solution)/shard_map/ppermute | solution.py:99
  39.0 1.0 collective-permute-done.2.refs_4_
  40.0 0.7 collective-permute-start.7
  40.6 1.7 collective-permute-done.7.refs_9_
  42.3 1.0 copy-done.6
  43.4 2.6 %pick.1 = (bf16[192,1792]{1,0:T(8,128)(2,1)S(1)}, bf16[192,1792]{1,0:T(8,128)(2,1)S(1)}, bf16[192,1792]{1,0:T(8,128)(2,1)S(1)}, bf16[192,1792]{1,0:T(8,128)(2,1)S(1)}, f32[32,128]{1,0:T(8,128)S(1)}) custom-call(s32[9]{0:T(128)S(1)} %copy-done.7, bf16[128,1920]{1,0:T(8,128)(2,1)S(1)} %copy-done.4, bf16[128,1920]{1,0:T(8,128)(2,1)S(1)} %copy-done.6, ...), custom_call_target="tpu_custom_call" | custom-call | flops 1 | bytes 1 | tf_op jit(solution)/shard_map/pick/pallas_call | solution.py:47
  46.0 1.3 collective-permute-start.11
  47.3 1.5 collective-permute-start.12
  48.8 1.6 products.3
  50.4 2.8 %collective-permute-start.9 = (bf16[3,96,1024]{2,1,0:T(8,128)(2,1)S(1)}, bf16[3,96,1024]{2,1,0:T(8,128)(2,1)S(1)}, u32[]{:S(2)}, u32[]{:S(2)}) collective-permute-start(bf16[3,96,1024]{2,1,0:T(8,128)(2,1)S(1)} %get-tuple-element.53), channel_id=1, source_target_pairs={{0,64},{32,224},{64,0},{96,160},{128,192},{160,96},{192,128},{224,... | collective-permute-start | bytes 1769480 | tf_op jit(solution)/shard_map/ppermute | solution.py:74
  53.2 7.6 %collective-permute-done.9.refs_1_ = bf16[3,96,1024]{2,1,0:T(8,128)(2,1)S(1)} collective-permute-done((bf16[3,96,1024]{2,1,0:T(8,128)(2,1)S(1)}, bf16[3,96,1024]{2,1,0:T(8,128)(2,1)S(1)}, u32[]{:S(2)}, u32[]{:S(2)}) %collective-permute-start.9) | collective-permute-done | bytes 589856 | tf_op jit(solution)/shard_map/ppermute | solution.py:74
  60.9 3.1 %collective-permute-done.11.refs_0_.refs_2_ = bf16[192,1792]{1,0:T(8,128)(2,1)S(1)} collective-permute-done((bf16[192,1792]{1,0:T(8,128)(2,1)S(1)}, bf16[192,1792]{1,0:T(8,128)(2,1)S(1)}, u32[]{:S(2)}, u32[]{:S(2)}) %collective-permute-start.11) | collective-permute-done | bytes 688160 | tf_op jit(solution)/shard_map/ppermute | solution.py:103
  63.9 2.6 %products.4 = (f32[3,192,1024]{2,1,0:T(8,128)S(1)}, bf16[3,192,1024]{2,1,0:T(8,128)(2,1)S(1)}) custom-call(bf16[192,1792]{1,0:T(8,128)(2,1)S(1)} %collective-permute-done.11.refs_0_.refs_2_, bf16[192,1792]{1,0:T(8,128)(2,1)S(1)} %collective-permute-done.12.refs_1_.refs_4_, bf16[2816,512]{1,0:T(8,128)(2,1)S(1)} %copy-done, ...), custom_call_target="tpu_custom_call" | custom-call | flops 1 | bytes 1 | tf_op jit(solution)/shard_map/products/pallas_call | solution.py:47
  66.6 2.8 %collective-permute-start.13 = (bf16[3,192,1024]{2,1,0:T(8,128)(2,1)S(1)}, bf16[3,192,1024]{2,1,0:T(8,128)(2,1)S(1)}, u32[]{:S(2)}, u32[]{:S(2)}) collective-permute-start(bf16[3,192,1024]{2,1,0:T(8,128)(2,1)S(1)} %get-tuple-element.59), channel_id=1, source_target_pairs={{0,64},{32,224},{64,0},{96,160},{128,192},{160,96},{192,128},{224,... | collective-permute-start | bytes 3538952 | tf_op jit(solution)/shard_map/ppermute | solution.py:74
  69.4 2.1 %collective-permute-start.14 = (bf16[192,1792]{1,0:T(8,128)(2,1)S(1)}, bf16[192,1792]{1,0:T(8,128)(2,1)S(1)}, u32[]{:S(2)}, u32[]{:S(2)}) collective-permute-start(bf16[192,1792]{1,0:T(8,128)(2,1)S(1)} %get-tuple-element.60), channel_id=1, source_target_pairs={{0,16},{8,24},{16,0},{24,8},{1,17},{9,25},{17,1},{25,9},{2,18},{10... | collective-permute-start | bytes 2064392 | tf_op jit(solution)/shard_map/ppermute | solution.py:103
  71.5 16.4 %collective-permute-done.14.refs_0_.refs_3_ = bf16[192,1792]{1,0:T(8,128)(2,1)S(1)} collective-permute-done((bf16[192,1792]{1,0:T(8,128)(2,1)S(1)}, bf16[192,1792]{1,0:T(8,128)(2,1)S(1)}, u32[]{:S(2)}, u32[]{:S(2)}) %collective-permute-start.14) | collective-permute-done | bytes 688160 | tf_op jit(solution)/shard_map/ppermute | solution.py:103
  87.9 1.6 products.5
  90.0 14.4 %collective-permute-done.16.refs_1_ = bf16[3,96,1024]{2,1,0:T(8,128)(2,1)S(1)} collective-permute-done((bf16[3,96,1024]{2,1,0:T(8,128)(2,1)S(1)}, bf16[3,96,1024]{2,1,0:T(8,128)(2,1)S(1)}, u32[]{:S(2)}, u32[]{:S(2)}) %collective-permute-start.16) | collective-permute-done | bytes 589856 | tf_op jit(solution)/shard_map/ppermute | solution.py:74
  104.9 2.1 %collective-permute-start.18 = (bf16[3,96,1024]{2,1,0:T(8,128)(2,1)S(1)}, bf16[3,96,1024]{2,1,0:T(8,128)(2,1)S(1)}, u32[]{:S(2)}, u32[]{:S(2)}) collective-permute-start(bf16[3,96,1024]{2,1,0:T(8,128)(2,1)S(1)} %terms.3.refs_4_.refs_0_.refs_9_), channel_id=1, source_target_pairs={{0,64},{32,224},{64,0},{96,160},{128,192},{160,96},{192,128},{224,... | collective-permute-start | bytes 1769480 | tf_op jit(solution)/shard_map/ppermute | solution.py:74
  107.0 0.5 collective-permute-start.23
  107.4 9.9 %collective-permute-done.17.refs_2_.refs_1_.refs_10_ = bf16[3,96,1024]{2,1,0:T(8,128)(2,1)S(1)} collective-permute-done((bf16[3,96,1024]{2,1,0:T(8,128)(2,1)S(1)}, bf16[3,96,1024]{2,1,0:T(8,128)(2,1)S(1)}, u32[]{:S(2)}, u32[]{:S(2)}) %collective-permute-start.17) | collective-permute-done | bytes 589856 | tf_op jit(solution)/shard_map/ppermute | solution.py:80
  117.4 0.7 collective-permute-start.22
  118.1 1.7 collective-permute-done.18.refs_3_.refs_2_.refs_11_
  119.9 3.5 %collective-permute-done.23.refs_1_ = bf16[3,48,1024]{2,1,0:T(8,128)(2,1)S(1)} collective-permute-done((bf16[3,48,1024]{2,1,0:T(8,128)(2,1)S(1)}, bf16[3,48,1024]{2,1,0:T(8,128)(2,1)S(1)}, u32[]{:S(2)}, u32[]{:S(2)}) %collective-permute-start.23) | collective-permute-done | bytes 294944 | tf_op jit(solution)/shard_map/ppermute | solution.py:80
  123.7 2.0 collective-permute-start.25
  125.7 1.5 collective-permute-start.20
  127.2 5.5 %collective-permute-done.24.refs_6_.refs_1_.refs_14_ = bf16[3,48,1024]{2,1,0:T(8,128)(2,1)S(1)} collective-permute-done((bf16[3,48,1024]{2,1,0:T(8,128)(2,1)S(1)}, bf16[3,48,1024]{2,1,0:T(8,128)(2,1)S(1)}, u32[]{:S(2)}, u32[]{:S(2)}) %collective-permute-start.24) | collective-permute-done | bytes 294944 | tf_op jit(solution)/shard_map/ppermute | solution.py:80
  132.7 0.8 collective-permute-start.28
  133.5 1.8 collective-permute-done.25.refs_7_.refs_2_.refs_15_
  135.3 1.8 back_rows.3
  137.1 1.3 collective-permute-start.26
  138.6 0.4 collective-permute-done.19.refs_6_.refs_1_
  139.0 2.6 %collective-permute-done.20.refs_7_.refs_2_ = bf16[3,48,1024]{2,1,0:T(8,128)(2,1)S(1)} collective-permute-done((bf16[3,48,1024]{2,1,0:T(8,128)(2,1)S(1)}, bf16[3,48,1024]{2,1,0:T(8,128)(2,1)S(1)}, u32[]{:S(2)}, u32[]{:S(2)}) %collective-permute-start.20) | collective-permute-done | bytes 294944 | tf_op jit(solution)/shard_map/ppermute | solution.py:74
  141.6 5.0 %collective-permute-done.28.refs_3_.refs_16_ = bf16[3,48,1024]{2,1,0:T(8,128)(2,1)S(1)} collective-permute-done((bf16[3,48,1024]{2,1,0:T(8,128)(2,1)S(1)}, bf16[3,48,1024]{2,1,0:T(8,128)(2,1)S(1)}, u32[]{:S(2)}, u32[]{:S(2)}) %collective-permute-start.28) | collective-permute-done | bytes 294944 | tf_op jit(solution)/shard_map/ppermute | solution.py:74
  146.5 1.3 back_rows.4.refs_8_
  147.9 1.5 collective-permute-start.29
  149.4 2.7 %collective-permute-start.21 = (bf16[3,48,1024]{2,1,0:T(8,128)(2,1)S(1)}, bf16[3,48,1024]{2,1,0:T(8,128)(2,1)S(1)}, u32[]{:S(2)}, u32[]{:S(2)}) collective-permute-start(bf16[3,48,1024]{2,1,0:T(8,128)(2,1)S(1)} %collective-permute-done.19.refs_6_.refs_1_), channel_id=1, source_target_pairs={{0,64},{32,224},{64,0},{96,160},{128,192},{160,96},{192,128},{224,... | collective-permute-start | bytes 884744 | tf_op jit(solution)/shard_map/ppermute | solution.py:74
  152.0 4.4 %collective-permute-done.21.refs_3_.refs_8_ = bf16[3,48,1024]{2,1,0:T(8,128)(2,1)S(1)} collective-permute-done((bf16[3,48,1024]{2,1,0:T(8,128)(2,1)S(1)}, bf16[3,48,1024]{2,1,0:T(8,128)(2,1)S(1)}, u32[]{:S(2)}, u32[]{:S(2)}) %collective-permute-start.21) | collective-permute-done | bytes 294944 | tf_op jit(solution)/shard_map/ppermute | solution.py:74
  156.5 1.3 back_rows.5.refs_2_.refs_6_
  157.8 0.5 collective-permute-done.29.refs_4_
  158.3 1.4 combine.1
  159.6 4.8 %collective-permute-start.30 = (bf16[448,896]{1,0:T(8,128)(2,1)S(1)}, bf16[448,896]{1,0:T(8,128)(2,1)S(1)}, u32[]{:S(2)}, u32[]{:S(2)}) collective-permute-start(bf16[448,896]{1,0:T(8,128)(2,1)S(1)} %get-tuple-element.71), channel_id=1, source_target_pairs={{0,32},{32,0},{1,33},{33,1},{2,34},{34,2},{3,35},{35,3},{4,36},{36... | collective-permute-start | bytes 2408456 | tf_op jit(solution)/shard_map/ppermute | solution.py:107
  164.5 1.9 collective-permute-done.30.refs_1_
  166.5 2.5 %collective-permute-start.31 = (bf16[128,896]{1,0:T(8,128)(2,1)S(1)}, bf16[128,896]{1,0:T(8,128)(2,1)S(1)}, u32[]{:S(2)}, u32[]{:S(2)}) collective-permute-start(bf16[128,896]{1,0:T(8,128)(2,1)S(1)} %get-tuple-element.72.refs_17_), channel_id=1, source_target_pairs={{0,7},{1,0},{2,1},{3,2},{4,3},{5,4},{6,5},{7,6},{32,33},{33,34},{3... | collective-permute-start | bytes 688136 | tf_op jit(solution)/shard_map/ppermute | solution.py:88
  169.1 3.9 %collective-permute-start.32 = (bf16[128,896]{1,0:T(8,128)(2,1)S(1)}, bf16[128,896]{1,0:T(8,128)(2,1)S(1)}, u32[]{:S(2)}, u32[]{:S(2)}) collective-permute-start(bf16[128,896]{1,0:T(8,128)(2,1)S(1)} %get-tuple-element.73), channel_id=1, source_target_pairs={{0,6},{1,7},{2,0},{3,1},{4,2},{5,3},{6,4},{7,5},{32,34},{33,35},{3... | collective-permute-start | bytes 688136 | tf_op jit(solution)/shard_map/ppermute | solution.py:88
  172.9 3.8 %collective-permute-start.34 = (bf16[64,896]{1,0:T(8,128)(2,1)S(1)}, bf16[64,896]{1,0:T(8,128)(2,1)S(1)}, u32[]{:S(2)}, u32[]{:S(2)}) collective-permute-start(bf16[64,896]{1,0:T(8,128)(2,1)S(1)} %get-tuple-element.75), channel_id=1, source_target_pairs={{0,4},{1,5},{2,6},{3,7},{4,0},{5,1},{6,2},{7,3},{32,36},{33,37},{3... | collective-permute-start | bytes 344072 | tf_op jit(solution)/shard_map/ppermute | solution.py:88
  176.7 9.1 %weight_grads.1 = (f32[8,128]{1,0:T(8,128)S(1)}, bf16[2,896,512]{2,1,0:T(8,128)(2,1)}, bf16[2,896,512]{2,1,0:T(8,128)(2,1)}, bf16[2,512,896]{2,1,0:T(8,128)(2,1)}, bf16[2816,512]{1,0:T(8,128)(2,1)}) custom-call(s32[9]{0:T(128)S(1)} %copy-done.7, bf16[192,1792]{1,0:T(8,128)(2,1)S(1)} %get-tuple-element.49.refs_0_.refs_3_.refs_1_, ...), custom_call_target="tpu_custom_call" | custom-call | flops 1 | bytes 1 | tf_op jit(solution)/shard_map/weight_grads/pallas_call | solution.py:47
  185.8 0.9 collective-permute-done.34.refs_5_
  186.7 3.4 %collective-permute-done.33.refs_4_ = bf16[128,896]{1,0:T(8,128)(2,1)S(1)} collective-permute-done((bf16[128,896]{1,0:T(8,128)(2,1)S(1)}, bf16[128,896]{1,0:T(8,128)(2,1)S(1)}, u32[]{:S(2)}, u32[]{:S(2)}) %collective-permute-start.33) | collective-permute-done | bytes 229408 | tf_op jit(solution)/shard_map/ppermute | solution.py:88
  190.0 0.7 bring_home.1
  190.7 6.1 %collective-permute-start.36 = (bf16[2816,512]{1,0:T(8,128)(2,1)}, bf16[2816,512]{1,0:T(8,128)(2,1)S(1)}, u32[]{:S(2)}, u32[]{:S(2)}) collective-permute-start(bf16[2816,512]{1,0:T(8,128)(2,1)} %get-tuple-element.80), channel_id=1, source_target_pairs={{0,32},{32,0},{1,33},{33,1},{2,34},{34,2},{3,35},{35,3},{4,36},{36... | collective-permute-start | bytes 8650760 | tf_op jit(solution)/shard_map/ppermute | solution.py:107
  196.9 5.3 %collective-permute-done.35.refs_1_ = f32[128,896]{1,0:T(8,128)S(1)} collective-permute-done((f32[128,896]{1,0:T(8,128)S(1)}, f32[128,896]{1,0:T(8,128)S(1)}, u32[]{:S(2)}, u32[]{:S(2)}) %collective-permute-start.35) | collective-permute-done | bytes 458784 | tf_op jit(solution)/shard_map/ppermute | solution.py:107
  202.2 0.8 finish.1
  203.0 2.1 %place_grads.1 = (bf16[2,896,512]{2,1,0:T(8,128)(2,1)}, bf16[2,896,512]{2,1,0:T(8,128)(2,1)}, bf16[2,512,896]{2,1,0:T(8,128)(2,1)}) custom-call(s32[9]{0:T(128)S(1)} %copy-done.7, bf16[2816,512]{1,0:T(8,128)(2,1)S(1)} %collective-permute-done.36.got, ...), custom_call_target="tpu_custom_call", output_to_operand_aliasing={{0}: (2, {}), {1}: (3, {}), {2}: (4, {})} | custom-call | bytes 6000000 | tf_op jit(solution)/shard_map/place_grads/pallas_call | solution.py:505
  (48 shorter events, 2.1 us)
Async XLA Ops:
  5.7 43.0 %collective-permute-start.8 = (bf16[2816,512]{1,0:T(8,128)(2,1)}, bf16[2816,512]{1,0:T(8,128)(2,1)S(1)}, u32[]{:S(2)}, u32[]{:S(2)}) collective-permute-start(bf16[2816,512]{1,0:T(8,128)(2,1)} %get-tuple-element.51), channel_id=1, source_target_pairs={{0,32},{32,0},{1,33},{33,1},{2,34},{34,2},{3,35},{35,3},{4,36},{36... | collective-permute-start | bytes 8650760 | tf_op jit(solution)/shard_map/ppermute | solution.py:107
  6.5 35.8 %copy-start.4 = (bf16[128,1920]{1,0:T(8,128)(2,1)S(1)}, bf16[128,1920]{1,0:T(8,128)(2,1)}, u32[]{:S(2)}) copy-start(bf16[128,1920]{1,0:T(8,128)(2,1)} %get-tuple-element.46.refs_1_.refs_10_) | copy-start | bytes 1474564
  6.5 35.8 %copy-start.7 = (s32[9]{0:T(128)S(1)}, s32[9]{0:T(128)}, u32[]{:S(2)}) copy-start(s32[9]{0:T(128)} %stack.39.refs_0_.info) | copy-start | bytes 112
  6.5 16.1 %collective-permute-start.1 = (bf16[128,1920]{1,0:T(8,128)(2,1)}, bf16[128,1920]{1,0:T(8,128)(2,1)}, u32[]{:S(2)}, u32[]{:S(2)}) collective-permute-start(bf16[128,1920]{1,0:T(8,128)(2,1)} %get-tuple-element.46.refs_1_.refs_10_), channel_id=1, source_target_pairs={{0,2},{1,3},{2,4},{3,5},{4,6},{5,7},{6,0},{7,1},{32,38},{33,39},{3... | collective-permute-start | bytes 1474568 | tf_op jit(solution)/shard_map/ppermute | solution.py:88
  11.6 17.1 %collective-permute-start = (bf16[128,1920]{1,0:T(8,128)(2,1)}, bf16[128,1920]{1,0:T(8,128)(2,1)S(1)}, u32[]{:S(2)}, u32[]{:S(2)}) collective-permute-start(bf16[128,1920]{1,0:T(8,128)(2,1)} %get-tuple-element.46.refs_1_.refs_10_), channel_id=1, source_target_pairs={{0,1},{1,2},{2,3},{3,4},{4,5},{5,6},{6,7},{7,0},{32,39},{33,32},{3... | collective-permute-start | bytes 1474568 | tf_op jit(solution)/shard_map/ppermute | solution.py:88
  22.6 13.9 %collective-permute-start.3 = (bf16[128,1920]{1,0:T(8,128)(2,1)}, bf16[128,1920]{1,0:T(8,128)(2,1)}, u32[]{:S(2)}, u32[]{:S(2)}) collective-permute-start(bf16[128,1920]{1,0:T(8,128)(2,1)} %collective-permute-done.1.refs_3_), channel_id=1, source_target_pairs={{0,2},{2,4},{4,6},{6,0},{33,39},{35,33},{37,35},{39,37},{8,10},{10... | collective-permute-start | bytes 1474568 | tf_op jit(solution)/shard_map/ppermute | solution.py:94
  28.6 11.4 %collective-permute-start.2 = (bf16[128,1920]{1,0:T(8,128)(2,1)}, bf16[128,1920]{1,0:T(8,128)(2,1)}, u32[]{:S(2)}, u32[]{:S(2)}) collective-permute-start(bf16[128,1920]{1,0:T(8,128)(2,1)} %collective-permute-done.1.refs_3_), channel_id=1, source_target_pairs={{0,1},{1,2},{2,3},{3,4},{4,5},{5,6},{6,7},{7,0},{32,39},{33,32},{3... | collective-permute-start | bytes 1474568 | tf_op jit(solution)/shard_map/ppermute | solution.py:88
  28.7 0.8 copy-start.5
  33.5 15.3 %copy-start = (bf16[2816,512]{1,0:T(8,128)(2,1)S(1)}, bf16[2816,512]{1,0:T(8,128)(2,1)}, u32[]{:S(2)}) copy-start(bf16[2816,512]{1,0:T(8,128)(2,1)} %get-tuple-element.50.refs_1_.refs_2_.refs_4_) | copy-start | bytes 8650756
  33.5 7.1 %collective-permute-start.5 = (bf16[128,1920]{1,0:T(8,128)(2,1)}, bf16[128,1920]{1,0:T(8,128)(2,1)S(1)}, u32[]{:S(2)}, u32[]{:S(2)}) collective-permute-start(bf16[128,1920]{1,0:T(8,128)(2,1)} %get-tuple-element.47.refs_2_), channel_id=1, source_target_pairs={{0,32},{32,0},{1,33},{33,1},{2,34},{34,2},{3,35},{35,3},{4,36},{36... | collective-permute-start | bytes 1474568 | tf_op jit(solution)/shard_map/ppermute | solution.py:107
  36.4 4.2 %collective-permute-start.6 = (bf16[128,1920]{1,0:T(8,128)(2,1)}, bf16[128,1920]{1,0:T(8,128)(2,1)S(1)}, u32[]{:S(2)}, u32[]{:S(2)}) collective-permute-start(bf16[128,1920]{1,0:T(8,128)(2,1)} %collective-permute-done.1.refs_3_), channel_id=1, source_target_pairs={{0,32},{32,0},{1,33},{33,1},{2,34},{34,2},{3,35},{35,3},{4,36},{36... | collective-permute-start | bytes 1474568 | tf_op jit(solution)/shard_map/ppermute | solution.py:107
  36.5 4.1 %collective-permute-start.4 = (bf16[128,1920]{1,0:T(8,128)(2,1)}, bf16[128,1920]{1,0:T(8,128)(2,1)S(1)}, u32[]{:S(2)}, u32[]{:S(2)}) collective-permute-start(bf16[128,1920]{1,0:T(8,128)(2,1)} %collective-permute-done.3.refs_5_), channel_id=1, source_target_pairs={{0,32},{33,1},{2,34},{35,3},{4,36},{37,5},{6,38},{39,7},{8,40},{41... | collective-permute-start | bytes 1474568 | tf_op jit(solution)/shard_map/ppermute | solution.py:99
  40.0 2.4 %collective-permute-start.7 = (bf16[128,1920]{1,0:T(8,128)(2,1)}, bf16[128,1920]{1,0:T(8,128)(2,1)S(1)}, u32[]{:S(2)}, u32[]{:S(2)}) collective-permute-start(bf16[128,1920]{1,0:T(8,128)(2,1)} %collective-permute-done.2.refs_4_), channel_id=1, source_target_pairs={{0,32},{32,0},{1,33},{33,1},{2,34},{34,2},{3,35},{35,3},{4,36},{36... | collective-permute-start | bytes 1474568 | tf_op jit(solution)/shard_map/ppermute | solution.py:107
  42.3 1.0 copy-start.6
  46.0 17.9 %collective-permute-start.11 = (bf16[192,1792]{1,0:T(8,128)(2,1)S(1)}, bf16[192,1792]{1,0:T(8,128)(2,1)S(1)}, u32[]{:S(2)}, u32[]{:S(2)}) collective-permute-start(bf16[192,1792]{1,0:T(8,128)(2,1)S(1)} %get-tuple-element.56), channel_id=1, source_target_pairs={{0,8},{8,16},{16,24},{24,0},{1,9},{9,17},{17,25},{25,1},{2,10},{10... | collective-permute-start | bytes 2064392 | tf_op jit(solution)/shard_map/ppermute | solution.py:103
  47.3 16.7 %collective-permute-start.12 = (bf16[192,1792]{1,0:T(8,128)(2,1)S(1)}, bf16[192,1792]{1,0:T(8,128)(2,1)S(1)}, u32[]{:S(2)}, u32[]{:S(2)}) collective-permute-start(bf16[192,1792]{1,0:T(8,128)(2,1)S(1)} %get-tuple-element.57), channel_id=1, source_target_pairs={{0,24},{8,0},{16,8},{24,16},{1,25},{9,1},{17,9},{25,17},{2,26},{10... | collective-permute-start | bytes 2064392 | tf_op jit(solution)/shard_map/ppermute | solution.py:103
  50.4 10.4 %collective-permute-start.9 = (bf16[3,96,1024]{2,1,0:T(8,128)(2,1)S(1)}, bf16[3,96,1024]{2,1,0:T(8,128)(2,1)S(1)}, u32[]{:S(2)}, u32[]{:S(2)}) collective-permute-start(bf16[3,96,1024]{2,1,0:T(8,128)(2,1)S(1)} %get-tuple-element.53), channel_id=1, source_target_pairs={{0,64},{32,224},{64,0},{96,160},{128,192},{160,96},{192,128},{224,... | collective-permute-start | bytes 1769480 | tf_op jit(solution)/shard_map/ppermute | solution.py:74
  63.9 2.6 %copy-start.2 = (bf16[192,1792]{1,0:T(8,128)(2,1)}, bf16[192,1792]{1,0:T(8,128)(2,1)S(1)}, u32[]{:S(2)}) copy-start(bf16[192,1792]{1,0:T(8,128)(2,1)S(1)} %collective-permute-done.11.refs_0_.refs_2_) | copy-start | bytes 2064388
  63.9 2.6 %copy-start.3 = (bf16[192,1792]{1,0:T(8,128)(2,1)}, bf16[192,1792]{1,0:T(8,128)(2,1)S(1)}, u32[]{:S(2)}) copy-start(bf16[192,1792]{1,0:T(8,128)(2,1)S(1)} %collective-permute-done.12.refs_1_.refs_4_) | copy-start | bytes 2064388
  66.6 23.1 %collective-permute-start.13 = (bf16[3,192,1024]{2,1,0:T(8,128)(2,1)S(1)}, bf16[3,192,1024]{2,1,0:T(8,128)(2,1)S(1)}, u32[]{:S(2)}, u32[]{:S(2)}) collective-permute-start(bf16[3,192,1024]{2,1,0:T(8,128)(2,1)S(1)} %get-tuple-element.59), channel_id=1, source_target_pairs={{0,64},{32,224},{64,0},{96,160},{128,192},{160,96},{192,128},{224,... | collective-permute-start | bytes 3538952 | tf_op jit(solution)/shard_map/ppermute | solution.py:74
  69.4 18.5 %collective-permute-start.14 = (bf16[192,1792]{1,0:T(8,128)(2,1)S(1)}, bf16[192,1792]{1,0:T(8,128)(2,1)S(1)}, u32[]{:S(2)}, u32[]{:S(2)}) collective-permute-start(bf16[192,1792]{1,0:T(8,128)(2,1)S(1)} %get-tuple-element.60), channel_id=1, source_target_pairs={{0,16},{8,24},{16,0},{24,8},{1,17},{9,25},{17,1},{25,9},{2,18},{10... | collective-permute-start | bytes 2064392 | tf_op jit(solution)/shard_map/ppermute | solution.py:103
  71.5 16.4 %collective-permute-start.10 = (bf16[3,48,1024]{2,1,0:T(8,128)(2,1)S(1)}, bf16[3,48,1024]{2,1,0:T(8,128)(2,1)S(1)}, u32[]{:S(2)}, u32[]{:S(2)}) collective-permute-start(bf16[3,48,1024]{2,1,0:T(8,128)(2,1)S(1)} %get-tuple-element.55), channel_id=1, source_target_pairs={{0,192},{32,96},{64,128},{96,32},{128,64},{160,224},{192,0},{224,1... | collective-permute-start | bytes 884744 | tf_op jit(solution)/shard_map/ppermute | solution.py:80
  87.9 1.6 copy-start.1
  89.6 14.9 %collective-permute-start.16 = (bf16[3,96,1024]{2,1,0:T(8,128)(2,1)S(1)}, bf16[3,96,1024]{2,1,0:T(8,128)(2,1)S(1)}, u32[]{:S(2)}, u32[]{:S(2)}) collective-permute-start(bf16[3,96,1024]{2,1,0:T(8,128)(2,1)S(1)} %get-tuple-element.64), channel_id=1, source_target_pairs={{0,64},{32,224},{64,0},{96,160},{128,192},{160,96},{192,128},{224,... | collective-permute-start | bytes 1769480 | tf_op jit(solution)/shard_map/ppermute | solution.py:74
  89.9 14.6 %collective-permute-start.15 = (bf16[3,96,1024]{2,1,0:T(8,128)(2,1)S(1)}, bf16[3,96,1024]{2,1,0:T(8,128)(2,1)S(1)}, u32[]{:S(2)}, u32[]{:S(2)}) collective-permute-start(bf16[3,96,1024]{2,1,0:T(8,128)(2,1)S(1)} %get-tuple-element.63), channel_id=1, source_target_pairs={{0,192},{32,96},{64,128},{96,32},{128,64},{160,224},{192,0},{224,1... | collective-permute-start | bytes 1769480 | tf_op jit(solution)/shard_map/ppermute | solution.py:80
  104.8 12.6 %collective-permute-start.17 = (bf16[3,96,1024]{2,1,0:T(8,128)(2,1)S(1)}, bf16[3,96,1024]{2,1,0:T(8,128)(2,1)S(1)}, u32[]{:S(2)}, u32[]{:S(2)}) collective-permute-start(bf16[3,96,1024]{2,1,0:T(8,128)(2,1)S(1)} %terms.3.refs_4_.refs_0_.refs_9_), channel_id=1, source_target_pairs={{0,192},{32,96},{64,128},{96,32},{128,64},{160,224},{192,0},{224,1... | collective-permute-start | bytes 1769480 | tf_op jit(solution)/shard_map/ppermute | solution.py:80
  104.9 14.8 %collective-permute-start.18 = (bf16[3,96,1024]{2,1,0:T(8,128)(2,1)S(1)}, bf16[3,96,1024]{2,1,0:T(8,128)(2,1)S(1)}, u32[]{:S(2)}, u32[]{:S(2)}) collective-permute-start(bf16[3,96,1024]{2,1,0:T(8,128)(2,1)S(1)} %terms.3.refs_4_.refs_0_.refs_9_), channel_id=1, source_target_pairs={{0,64},{32,224},{64,0},{96,160},{128,192},{160,96},{192,128},{224,... | collective-permute-start | bytes 1769480 | tf_op jit(solution)/shard_map/ppermute | solution.py:74
  107.0 16.4 %collective-permute-start.23 = (bf16[3,48,1024]{2,1,0:T(8,128)(2,1)S(1)}, bf16[3,48,1024]{2,1,0:T(8,128)(2,1)S(1)}, u32[]{:S(2)}, u32[]{:S(2)}) collective-permute-start(bf16[3,48,1024]{2,1,0:T(8,128)(2,1)S(1)} %get-tuple-element.66), channel_id=1, source_target_pairs={{0,192},{32,96},{64,128},{96,32},{128,64},{160,224},{192,0},{224,1... | collective-permute-start | bytes 884744 | tf_op jit(solution)/shard_map/ppermute | solution.py:80
  117.4 17.9 %collective-permute-start.22 = (bf16[3,96,1024]{2,1,0:T(8,128)(2,1)S(1)}, bf16[3,96,1024]{2,1,0:T(8,128)(2,1)S(1)}, u32[]{:S(2)}, u32[]{:S(2)}) collective-permute-start(bf16[3,96,1024]{2,1,0:T(8,128)(2,1)S(1)} %collective-permute-done.17.refs_2_.refs_1_.refs_10_), channel_id=1, source_target_pairs={{0,64},{32,224},{64,0},{96,160},{128,192},{160,96},{192,128},{224,... | collective-permute-start | bytes 1769480 | tf_op jit(solution)/shard_map/ppermute | solution.py:74
  123.6 9.1 %collective-permute-start.24 = (bf16[3,48,1024]{2,1,0:T(8,128)(2,1)S(1)}, bf16[3,48,1024]{2,1,0:T(8,128)(2,1)S(1)}, u32[]{:S(2)}, u32[]{:S(2)}) collective-permute-start(bf16[3,48,1024]{2,1,0:T(8,128)(2,1)S(1)} %terms.5.refs_8_.refs_0_.refs_13_), channel_id=1, source_target_pairs={{0,192},{32,96},{64,128},{96,32},{128,64},{160,224},{192,0},{224,1... | collective-permute-start | bytes 884744 | tf_op jit(solution)/shard_map/ppermute | solution.py:80
  123.7 11.6 %collective-permute-start.25 = (bf16[3,48,1024]{2,1,0:T(8,128)(2,1)S(1)}, bf16[3,48,1024]{2,1,0:T(8,128)(2,1)S(1)}, u32[]{:S(2)}, u32[]{:S(2)}) collective-permute-start(bf16[3,48,1024]{2,1,0:T(8,128)(2,1)S(1)} %terms.5.refs_8_.refs_0_.refs_13_), channel_id=1, source_target_pairs={{0,64},{32,224},{64,0},{96,160},{128,192},{160,96},{192,128},{224,... | collective-permute-start | bytes 884744 | tf_op jit(solution)/shard_map/ppermute | solution.py:74
  125.7 13.3 %collective-permute-start.19 = (bf16[3,48,1024]{2,1,0:T(8,128)(2,1)S(1)}, bf16[3,48,1024]{2,1,0:T(8,128)(2,1)S(1)}, u32[]{:S(2)}, u32[]{:S(2)}) collective-permute-start(bf16[3,48,1024]{2,1,0:T(8,128)(2,1)S(1)} %terms.4.refs_2_.refs_0_.refs_5_), channel_id=1, source_target_pairs={{0,192},{32,96},{64,128},{96,32},{128,64},{160,224},{192,0},{224,1... | collective-permute-start | bytes 884744 | tf_op jit(solution)/shard_map/ppermute | solution.py:80
  125.7 15.9 %collective-permute-start.20 = (bf16[3,48,1024]{2,1,0:T(8,128)(2,1)S(1)}, bf16[3,48,1024]{2,1,0:T(8,128)(2,1)S(1)}, u32[]{:S(2)}, u32[]{:S(2)}) collective-permute-start(bf16[3,48,1024]{2,1,0:T(8,128)(2,1)S(1)} %terms.4.refs_2_.refs_0_.refs_5_), channel_id=1, source_target_pairs={{0,64},{32,224},{64,0},{96,160},{128,192},{160,96},{192,128},{224,... | collective-permute-start | bytes 884744 | tf_op jit(solution)/shard_map/ppermute | solution.py:74
  132.7 13.9 %collective-permute-start.28 = (bf16[3,48,1024]{2,1,0:T(8,128)(2,1)S(1)}, bf16[3,48,1024]{2,1,0:T(8,128)(2,1)S(1)}, u32[]{:S(2)}, u32[]{:S(2)}) collective-permute-start(bf16[3,48,1024]{2,1,0:T(8,128)(2,1)S(1)} %collective-permute-done.24.refs_6_.refs_1_.refs_14_), channel_id=1, source_target_pairs={{0,64},{32,224},{64,0},{96,160},{128,192},{160,96},{192,128},{224,... | collective-permute-start | bytes 884744 | tf_op jit(solution)/shard_map/ppermute | solution.py:74
  137.1 19.4 %collective-permute-start.26 = (bf16[192,896]{1,0:T(8,128)(2,1)S(1)}, bf16[192,896]{1,0:T(8,128)(2,1)S(1)}, u32[]{:S(2)}, u32[]{:S(2)}) collective-permute-start(bf16[192,896]{1,0:T(8,128)(2,1)S(1)} %get-tuple-element.67.refs_8_), channel_id=1, source_target_pairs={{0,24},{8,0},{16,8},{24,16},{1,25},{9,1},{17,9},{25,17},{2,26},{10... | collective-permute-start | bytes 1032200 | tf_op jit(solution)/shard_map/ppermute | solution.py:103
  138.4 18.1 %collective-permute-start.27 = (bf16[192,896]{1,0:T(8,128)(2,1)S(1)}, bf16[192,896]{1,0:T(8,128)(2,1)S(1)}, u32[]{:S(2)}, u32[]{:S(2)}) collective-permute-start(bf16[192,896]{1,0:T(8,128)(2,1)S(1)} %get-tuple-element.68), channel_id=1, source_target_pairs={{0,8},{8,16},{16,24},{24,0},{1,9},{9,17},{17,25},{25,1},{2,10},{10... | collective-permute-start | bytes 1032200 | tf_op jit(solution)/shard_map/ppermute | solution.py:103
  147.9 10.4 %collective-permute-start.29 = (bf16[192,896]{1,0:T(8,128)(2,1)S(1)}, bf16[192,896]{1,0:T(8,128)(2,1)S(1)}, u32[]{:S(2)}, u32[]{:S(2)}) collective-permute-start(bf16[192,896]{1,0:T(8,128)(2,1)S(1)} %back_rows.4.refs_8_), channel_id=1, source_target_pairs={{0,16},{8,24},{16,0},{24,8},{1,17},{9,25},{17,1},{25,9},{2,18},{10... | collective-permute-start | bytes 1032200 | tf_op jit(solution)/shard_map/ppermute | solution.py:103
  149.4 7.1 %collective-permute-start.21 = (bf16[3,48,1024]{2,1,0:T(8,128)(2,1)S(1)}, bf16[3,48,1024]{2,1,0:T(8,128)(2,1)S(1)}, u32[]{:S(2)}, u32[]{:S(2)}) collective-permute-start(bf16[3,48,1024]{2,1,0:T(8,128)(2,1)S(1)} %collective-permute-done.19.refs_6_.refs_1_), channel_id=1, source_target_pairs={{0,64},{32,224},{64,0},{96,160},{128,192},{160,96},{192,128},{224,... | collective-permute-start | bytes 884744 | tf_op jit(solution)/shard_map/ppermute | solution.py:74
  159.6 6.7 %collective-permute-start.30 = (bf16[448,896]{1,0:T(8,128)(2,1)S(1)}, bf16[448,896]{1,0:T(8,128)(2,1)S(1)}, u32[]{:S(2)}, u32[]{:S(2)}) collective-permute-start(bf16[448,896]{1,0:T(8,128)(2,1)S(1)} %get-tuple-element.71), channel_id=1, source_target_pairs={{0,32},{32,0},{1,33},{33,1},{2,34},{34,2},{3,35},{35,3},{4,36},{36... | collective-permute-start | bytes 2408456 | tf_op jit(solution)/shard_map/ppermute | solution.py:107
  166.5 20.1 %collective-permute-start.31 = (bf16[128,896]{1,0:T(8,128)(2,1)S(1)}, bf16[128,896]{1,0:T(8,128)(2,1)S(1)}, u32[]{:S(2)}, u32[]{:S(2)}) collective-permute-start(bf16[128,896]{1,0:T(8,128)(2,1)S(1)} %get-tuple-element.72.refs_17_), channel_id=1, source_target_pairs={{0,7},{1,0},{2,1},{3,2},{4,3},{5,4},{6,5},{7,6},{32,33},{33,34},{3... | collective-permute-start | bytes 688136 | tf_op jit(solution)/shard_map/ppermute | solution.py:88
  169.1 17.6 %collective-permute-start.32 = (bf16[128,896]{1,0:T(8,128)(2,1)S(1)}, bf16[128,896]{1,0:T(8,128)(2,1)S(1)}, u32[]{:S(2)}, u32[]{:S(2)}) collective-permute-start(bf16[128,896]{1,0:T(8,128)(2,1)S(1)} %get-tuple-element.73), channel_id=1, source_target_pairs={{0,6},{1,7},{2,0},{3,1},{4,2},{5,3},{6,4},{7,5},{32,34},{33,35},{3... | collective-permute-start | bytes 688136 | tf_op jit(solution)/shard_map/ppermute | solution.py:88
  172.9 17.1 %collective-permute-start.33 = (bf16[128,896]{1,0:T(8,128)(2,1)S(1)}, bf16[128,896]{1,0:T(8,128)(2,1)S(1)}, u32[]{:S(2)}, u32[]{:S(2)}) collective-permute-start(bf16[128,896]{1,0:T(8,128)(2,1)S(1)} %get-tuple-element.74), channel_id=1, source_target_pairs={{0,5},{1,6},{2,7},{3,0},{4,1},{5,2},{6,3},{7,4},{32,35},{33,36},{3... | collective-permute-start | bytes 688136 | tf_op jit(solution)/shard_map/ppermute | solution.py:88
  172.9 13.7 %collective-permute-start.34 = (bf16[64,896]{1,0:T(8,128)(2,1)S(1)}, bf16[64,896]{1,0:T(8,128)(2,1)S(1)}, u32[]{:S(2)}, u32[]{:S(2)}) collective-permute-start(bf16[64,896]{1,0:T(8,128)(2,1)S(1)} %get-tuple-element.75), channel_id=1, source_target_pairs={{0,4},{1,5},{2,6},{3,7},{4,0},{5,1},{6,2},{7,3},{32,36},{33,37},{3... | collective-permute-start | bytes 344072 | tf_op jit(solution)/shard_map/ppermute | solution.py:88
  190.7 12.3 %collective-permute-start.36 = (bf16[2816,512]{1,0:T(8,128)(2,1)}, bf16[2816,512]{1,0:T(8,128)(2,1)S(1)}, u32[]{:S(2)}, u32[]{:S(2)}) collective-permute-start(bf16[2816,512]{1,0:T(8,128)(2,1)} %get-tuple-element.80), channel_id=1, source_target_pairs={{0,32},{32,0},{1,33},{33,1},{2,34},{34,2},{3,35},{35,3},{4,36},{36... | collective-permute-start | bytes 8650760 | tf_op jit(solution)/shard_map/ppermute | solution.py:107
  196.8 5.4 %collective-permute-start.35 = (f32[128,896]{1,0:T(8,128)S(1)}, f32[128,896]{1,0:T(8,128)S(1)}, u32[]{:S(2)}, u32[]{:S(2)}) collective-permute-start(f32[128,896]{1,0:T(8,128)S(1)} %get-tuple-element.78.refs_0_.refs_2_), channel_id=1, source_target_pairs={{0,32},{32,0},{1,33},{33,1},{2,34},{34,2},{3,35},{35,3},{4,36},{36... | collective-permute-start | bytes 1376264 | tf_op jit(solution)/shard_map/ppermute | solution.py:107
